TPU v7x, 256 devices: a whole 4x4x8 slice. The times are simulated.
256 devices in a mesh: dp: 64 (over y_lo, z, x), tensor: 4 (over y_hi, core).
Axes of the slice: x: 4, y: 4 (y_hi: 2, y_lo: 2; y = y_hi * 2 + y_lo), z: 8, core: 2. Of those that a mesh axis runs over, the one named last changes fastest.
Arguments:
- hidden: bfloat16 [10240, 14336], P('dp', 'tensor'), may hold values from -6 to 6
- out_grad: bfloat16 [10240, 4096], P('dp', 'tensor'), may hold values from -16 to 16
- weight: bfloat16 [4096, 14336], P('dp', 'tensor'), may hold values from -0.09375 to 0.09375
Outputs:
- hidden_grad: bfloat16 [10240, 14336], P('dp', 'tensor')
- weight_grad: float32 [4096, 14336], P('dp', 'tensor')
All inputs are finite; a program needn't handle non-finite values.
Results may differ from a plain program's by a relative error of at most 0.001.
Values may be sent and summed in bfloat16 or wider, within the bound.
A program may use at most 256 MiB of HBM per device.

v0:
```python
import jax
import jax.numpy as jnp
from jax import lax
from jax.sharding import PartitionSpec as P


def shards(hidden, out_grad, weight):
    full_grad = lax.all_gather(out_grad, "tensor", axis=1, tiled=True)
    columns = full_grad
    hidden_grad = jnp.dot(
        columns,
        lax.all_gather(weight, "dp", axis=0, tiled=True),
        preferred_element_type=jnp.float32,
    ).astype(jnp.bfloat16)
    columns = full_grad
    weight_grad = lax.psum_scatter(
        lax.dot_general(
            columns, hidden, (((0,), (0,)), ((), ())), preferred_element_type=jnp.float32
        ),
        "dp",
        scatter_dimension=0,
        tiled=True,
    )
    return (hidden_grad, weight_grad)


def solution(mesh):
    return jax.shard_map(
        shards,
        mesh=mesh,
        in_specs=(P("dp", "tensor"), P("dp", "tensor"), P("dp", "tensor")),
        out_specs=(P("dp", "tensor"), P("dp", "tensor")),
        check_vma=False,
    )
```

profile of v0, /device:TPU:1, one launch (start us, length us, event | category | flops | bytes accessed | tf_op | source)
XLA Modules:
  0.0 1043.0 jit_solution(16930245739939941886)
XLA Ops:
  7.2 0.0 copy-start
  7.2 0.0 all-gather.3.cloned.1.call-start
  7.2 0.7 all-gather.3.cloned.1.call-update
  7.9 0.0 all-gather.5.cloned.1.call-start
  8.0 0.7 all-gather.5.cloned.1.call-update
  8.7 0.0 reduce-scatter.2.cloned.1.call-start
  8.7 30.2 %all-gather.3.cloned.1.call-done = bf16[160,4096]{1,0:T(8,128)(2,1)} async-done(((bf16[160,1024]{1,0:T(8,128)(2,1)}), bf16[160,4096]{1,0:T(8,128)(2,1)}) %all-gather.3.cloned.1.call-update) | async-done | bytes 1310736 | tf_op jit(solution)/shard_map/all_gather | solution.py:8
  38.9 0.0 copy-done
  38.9 24.2 %fusion = f32[4096,3584]{1,0:T(8,128)} fusion(bf16[160,4096]{1,0:T(8,128)(2,1)} %all-gather.3.cloned.1.call-done, bf16[160,3584]{1,0:T(8,128)(2,1)S(1)} %copy-done), kind=kOutput, calls=%fused_computation.1 | convolution fusion | flops 4697620480 | bytes 61177856 | tf_op jit(solution)/shard_map/dot_general | solution.py:17
  63.0 0.0 copy-start.2
  63.0 0.0 reduce-scatter.2.cloned.1.call-update
  63.1 306.1 %all-gather.5.cloned.1.call-done = bf16[4096,3584]{1,0:T(8,128)(2,1)} async-done(((bf16[64,3584]{1,0:T(8,128)(2,1)}), bf16[4096,3584]{1,0:T(8,128)(2,1)}) %all-gather.5.cloned.1.call-update) | async-done | bytes 29360144 | tf_op jit(solution)/shard_map/all_gather | solution.py:12
  369.1 0.0 copy-done.2
  369.1 0.0 copy-start.1
  369.1 13.1 %convolution_convert_fusion = bf16[160,3584]{1,0:T(8,128)(2,1)} fusion(bf16[160,4096]{1,0:T(8,128)(2,1)S(1)} %copy-done.2, bf16[4096,3584]{1,0:T(8,128)(2,1)} %all-gather.5.cloned.1.call-done), kind=kOutput, calls=%fused_computation | convolution fusion | flops 4698193920 | bytes 31817728 | tf_op jit(solution)/shard_map/dot_general | solution.py:10
  382.2 654.2 %reduce-scatter.2.cloned.1.call-done = f32[64,3584]{1,0:T(8,128)} async-done(((f32[4096,3584]{1,0:T(8,128)}), f32[64,3584]{1,0:T(8,128)}) %reduce-scatter.2.cloned.1.call-update) | async-done | bytes 917520 | tf_op jit(solution)/shard_map/reduce_scatter | solution.py:16
  1036.5 0.0 copy-done.1
Async XLA Ops:
  7.2 31.7 %copy-start = (bf16[160,3584]{1,0:T(8,128)(2,1)S(1)}, bf16[160,3584]{1,0:T(8,128)(2,1)}, u32[]{:S(2)}) copy-start(bf16[160,3584]{1,0:T(8,128)(2,1)} %param.3) | copy-start | bytes 3440644
  7.2 31.7 %all-gather.3.cloned.1.call-start = ((), (), s32[]{:S(2)}) async-start(), calls=%async_computation.1 | async-start | bytes 1638400 | tf_op jit(solution)/shard_map/all_gather | solution.py:8
  7.9 361.2 %all-gather.5.cloned.1.call-start = ((), (), s32[]{:S(2)}) async-start(), calls=%async_computation.2 | async-start | bytes 29818880 | tf_op jit(solution)/shard_map/all_gather | solution.py:12
  8.7 1027.8 %reduce-scatter.2.cloned.1.call-start = ((), (), s32[]{:S(2)}) async-start(), calls=%async_computation.3 | async-start | bytes 59637760 | tf_op jit(solution)/shard_map/reduce_scatter | solution.py:16
  63.0 306.1 %copy-start.2 = (bf16[160,4096]{1,0:T(8,128)(2,1)S(1)}, bf16[160,4096]{1,0:T(8,128)(2,1)}, u32[]{:S(2)}) copy-start(bf16[160,4096]{1,0:T(8,128)(2,1)} %all-gather.3.cloned.1.call-done) | copy-start | bytes 3932164
  369.1 667.3 %copy-start.1 = (bf16[160,3584]{1,0:T(8,128)(2,1)S(1)}, bf16[160,3584]{1,0:T(8,128)(2,1)}, u32[]{:S(2)}) copy-start(bf16[160,3584]{1,0:T(8,128)(2,1)} %param.3) | copy-start | bytes 3440644
Sparse Core Ops, SparseCore 0:
  9.8 28.9 all-gather.2
  40.7 328.4 all-gather.4
  372.3 664.1 reduce-scatter.1
where the time goes:
time: 1040 us
  waiting for transfers between devices  992 us (95%)
  matrix products  37.3 us (4%)
  between operations  13.8 us (1%)
    reduce_scatter x1, waiting for transfers between devices, shards(): lax.psum_scatter(lax.dot_general(columns, hidden, (((0,), (0,)), ((), ())...  654 us
    all_gather x1, waiting for transfers between devices, shards(): lax.all_gather(weight, 'dp', axis=0, tiled=True)  306 us
    all_gather x1, waiting for transfers between devices, shards(): full_grad = lax.all_gather(out_grad, 'tensor', axis=1, tiled=True)  30.2 us
    dot_general x1, matrix products, shards(): lax.dot_general(columns, hidden, (((0,), (0,)), ((), ())), preferred_elem...  24.2 us
  transfers between devices with their start and end apart: 3, of which 3 were waited for; matrix products, arithmetic and copies ran while one was open for 4% of the time, Pallas kernels for 0%

commit v1 on v0

v1 whole, which is shorter than its diff:
```python
import jax
import jax.numpy as jnp
from jax import lax
from jax.experimental import pallas as pl
from jax.experimental.pallas import tpu as pltpu
from jax.sharding import PartitionSpec as P

MESH = pl.DeviceIdType.MESH
LANES = 128
BASE = pl.ds(0, 3 * LANES)
EXTRA = pl.ds(3 * LANES, LANES)
WIDE = 4 * LANES
T = 160
F = 64
G = 1024
Q = 256
CHUNK = 32
TOP = 32768.0


def aligned(value, step):
    return pl.multiple_of(value, step)


def encode(total, scale):
    t = total * scale
    t2 = t * t
    t4 = t2 * t2
    t8 = t4 * t4
    return jnp.where(t < 0, -t8, t8).astype(jnp.bfloat16)


def decode(code, scale):
    y = code.astype(jnp.float32)
    root = lax.rsqrt(lax.rsqrt(jnp.maximum(jnp.abs(y), 1e-37)))
    root = root * lax.rsqrt(root)
    return jnp.where(y < 0, -root, root) * scale


def kernel(
    hidden, grad, weight, hg_out, wg_out,
    og, w, hid, rs_send, rs_recv, acc, stage_h, stage_w,
    loc, w_s, w_r, h_s, h_r, g_s, g_r, o_s, o_r,
    a_s, a_r, b_s, b_r, s_s, s_r, z_s, z_r, r_s, r_r,
):
    dp, tensor = lax.axis_index("dp"), lax.axis_index("tensor")
    x, z, y_lo = lax.rem(dp, 4), lax.rem(lax.div(dp, 4), 8), lax.div(dp, 32)
    y_hi, core = lax.div(tensor, 2), lax.rem(tensor, 2)
    y, j = y_hi * 2 + y_lo, y_lo * 4 + x

    def device(xx, yy, zz, cc):
        return ((lax.rem(yy, 2) * 8 + zz) * 4 + xx, lax.div(yy, 2) * 2 + cc)

    def four(jj):
        return lax.rem(jj + core, 2) == 0

    def first(jj):
        return lax.div(7 * jj + 1 - core, 2) * LANES

    def partner(r):
        xx, yl = lax.rem(x + lax.rem(r, 4), 4), lax.rem(y_lo + lax.div(r, 4), 2)
        return yl * 4 + xx, device(xx, y_hi * 2 + yl, z, core)

    mine4 = four(j)
    my_first = first(j)
    sibling = device(x, y, z, 1 - core)

    barrier = pltpu.get_barrier_semaphore()
    greeted = [partner(r)[1] for r in range(1, 8)]
    greeted += [device(x, y, lax.rem(z + 1, 8), core), device(x, y, lax.rem(z + 7, 8), core)]
    greeted += [sibling, device(x, 3 - y, z, core)]
    for dev in greeted:
        pl.semaphore_signal(barrier, inc=1, device_id=dev, device_id_type=MESH)
    pl.semaphore_wait(barrier, len(greeted))

    pending = []

    def remote(src, dst, ss, rs, dev):
        return pltpu.make_async_remote_copy(
            src_ref=src, dst_ref=dst, send_sem=ss, recv_sem=rs, device_id=dev, device_id_type=MESH
        )

    def send(src, dst, ss, rs, dev, cond=None):
        copy = remote(src, dst, ss, rs, dev)
        if cond is None:
            copy.start()
        else:
            pl.when(cond)(copy.start)
        pending.append((cond, copy))

    def arrived(ref, sem, cond=None):
        copy = pltpu.make_async_copy(ref, ref, sem)
        if cond is None:
            copy.wait()
        else:
            pl.when(cond)(copy.wait)

    def local(src, dst, sem, cond=None):
        copy = pltpu.make_async_copy(src, dst, sem)
        if cond is None:
            copy.start()
        else:
            pl.when(cond)(copy.start)

    w_rows = pl.ds(aligned(z * Q + x * F, F), F)
    for r in (2, 6, 1, 3, 5, 7, 4):
        jj, dev = partner(r)
        c = aligned(first(jj), LANES)
        send(weight.at[:, pl.ds(c, 3 * LANES)], w.at[y_lo, w_rows, BASE], w_s.at[r, 0], w_r.at[y_lo, 0], dev)
        send(
            weight.at[:, pl.ds(c + 3 * LANES, LANES)], w.at[y_lo, w_rows, EXTRA],
            w_s.at[r, 1], w_r.at[y_lo, 1], dev, four(jj),
        )
    c = aligned(my_first, LANES)
    local(weight.at[:, pl.ds(c, 3 * LANES)], w.at[y_lo, w_rows, BASE], w_r.at[y_lo, 0])
    local(weight.at[:, pl.ds(c + 3 * LANES, LANES)], w.at[y_lo, w_rows, EXTRA], w_r.at[y_lo, 1], mine4)

    a, b = x * (1 - core) + y * core, x * core + y * (1 - core)

    def place(aa, bb):
        aa, bb = lax.rem(aa, 4), lax.rem(bb, 4)
        return aa * (1 - core) + bb * core, aa * core + bb * (1 - core)

    def block(da, db, half=None):
        xx, yy = place(a + da, b + db)
        row = (lax.rem(yy, 2) * 4 + xx) * T
        rows = pl.ds(aligned(row, 32), T) if half is None else pl.ds(aligned(row + half * (T // 2), 16), T // 2)
        return og.at[lax.div(yy, 2), core, rows, :]

    def towards(da, db):
        xx, yy = place(a + da, b + db)
        return device(xx, yy, z, core)

    def pass_on(da, db):
        i = da * 4 + db
        src = grad if i == 0 else block(da, db)
        send(src, block(da, db), s_s.at[i], s_r.at[0], sibling)

    def b_start(da):
        src = grad if da == 0 else block(da, 0)
        send(src, block(da, 0), b_s.at[da, 0], b_r.at[da, 0], towards(0, 1))
        send(src, block(da, 0), b_s.at[da, 1], b_r.at[da, 1], towards(0, 3))

    def b_forward(da):
        arrived(block(da, 3), b_r.at[da, 0])
        send(block(da, 3, 0), block(da, 3, 0), b_s.at[da, 2], b_r.at[da, 2], towards(0, 1))
        arrived(block(da, 1), b_r.at[da, 1])
        send(block(da, 1, 1), block(da, 1, 1), b_s.at[da, 3], b_r.at[da, 3], towards(0, 3))
        pass_on(da, 3)
        pass_on(da, 1)

    def b_last(da):
        arrived(block(da, 2, 0), b_r.at[da, 2])
        arrived(block(da, 2, 1), b_r.at[da, 3])
        pass_on(da, 2)

    z_next = (device(x, y, lax.rem(z + 1, 8), core), device(x, y, lax.rem(z + 7, 8), core))

    def z_rows(plane):
        return pl.ds(aligned(lax.rem(plane + 8, 8) * Q, Q), Q)

    def z_send(s, way, h):
        plane = z - s + 1 if way == 0 else z + s - 1
        for i, cols in enumerate((BASE, EXTRA)):
            ref = w.at[h, z_rows(plane), cols]
            send(ref, ref, z_s.at[way, s - 1, h, i], z_r.at[way, s - 1, h, i], z_next[way], mine4 if i else None)

    def z_wait(s, way, h):
        plane = z - s if way == 0 else z + s
        arrived(w.at[h, z_rows(plane), BASE], z_r.at[way, s - 1, h, 0])
        arrived(w.at[h, z_rows(plane), EXTRA], z_r.at[way, s - 1, h, 1], mine4)

    def z_step(s, h):
        for way in (0, 1):
            z_wait(s, way, h)
            if s < 3 or way == h:
                z_send(s + 1, way, h)

    send(grad, block(0, 0), a_s.at[0], a_r.at[0], towards(1, 0))
    send(grad, block(0, 0), a_s.at[1], a_r.at[1], towards(3, 0))
    b_start(0)
    local(grad, block(0, 0), loc.at[0])
    pass_on(0, 0)

    h_rows = pl.ds(aligned(j * T, 32), T)
    for r in (2, 6, 1, 3, 5, 7, 4):
        jj, dev = partner(r)
        c = aligned(first(jj), LANES)
        send(hidden.at[:, pl.ds(c, 3 * LANES)], hid.at[h_rows, BASE], h_s.at[r, 0], h_r.at[0], dev)
        send(
            hidden.at[:, pl.ds(c + 3 * LANES, LANES)], hid.at[h_rows, EXTRA],
            h_s.at[r, 1], h_r.at[1], dev, four(jj),
        )
    c = aligned(my_first, LANES)
    local(hidden.at[:, pl.ds(c, 3 * LANES)], hid.at[h_rows, BASE], h_r.at[0])
    local(hidden.at[:, pl.ds(c + 3 * LANES, LANES)], hid.at[h_rows, EXTRA], h_r.at[1], mine4)

    for h in (0, 1):
        arrived(w.at[h, z_rows(z), BASE], w_r.at[h, 0])
        arrived(w.at[h, z_rows(z), EXTRA], w_r.at[h, 1], mine4)
        for way in (0, 1):
            z_send(1, way, h)

    arrived(block(3, 0), a_r.at[0])
    send(block(3, 0, 0), block(3, 0, 0), a_s.at[2], a_r.at[2], towards(1, 0))
    arrived(block(1, 0), a_r.at[1])
    send(block(1, 0, 1), block(1, 0, 1), a_s.at[3], a_r.at[3], towards(3, 0))
    b_start(3)
    b_start(1)
    pass_on(3, 0)
    pass_on(1, 0)
    b_forward(0)
    z_step(1, 0)
    arrived(block(2, 0, 0), a_r.at[2])
    arrived(block(2, 0, 1), a_r.at[3])
    b_start(2)
    pass_on(2, 0)
    z_step(1, 1)
    b_forward(3)
    z_step(2, 0)
    b_forward(1)
    b_last(0)
    z_step(2, 1)
    b_forward(2)
    b_last(3)
    z_step(3, 0)
    b_last(1)
    b_last(2)
    z_step(3, 1)

    arrived(grad, loc.at[0])
    arrived(og.at[:, 1 - core], s_r.at[0])
    arrived(hid.at[:, BASE], h_r.at[0])
    arrived(hid.at[:, EXTRA], h_r.at[1], mine4)

    def product(h, d):
        lhs = og[h, lax.div(d, 4), :, pl.ds(aligned(lax.rem(d, 4) * Q, Q), Q)]
        acc[...] = lax.dot_general(lhs, hid[...], (((0,), (0,)), ((), ())), preferred_element_type=jnp.float32)

    def add(way, k):
        scale = rs_recv[way, k, Q : Q + 16, :].astype(jnp.float32)[0:1, :] * (1.0 / TOP)

        def rows(i, carry):
            at = pl.ds(aligned(i * CHUNK, CHUNK), CHUNK)
            acc[at, :] += decode(rs_recv[way, k, at, :], scale)
            return carry

        lax.fori_loop(0, Q // CHUNK, rows, 0)

    def rs_wait(way, k):
        arrived(rs_recv.at[way, k, :, BASE], r_r.at[way, k, 0])
        arrived(rs_recv.at[way, k, :, EXTRA], r_r.at[way, k, 1], mine4)

    def rs_copy(way, k, i):
        cols = (BASE, EXTRA)[i]
        to = device(x, y, lax.rem(z + 1 + 6 * way, 8), core)
        return remote(rs_send.at[way, k, :, cols], rs_recv.at[way, k, :, cols], r_s.at[way, k, i], r_r.at[way, k, i], to)

    def rs_one(k, way):
        s, odd = lax.div(k + 3, 2), lax.rem(k, 2)
        h = way + odd - 2 * way * odd
        d = lax.rem(z + 8 + (1 - 2 * way) * (5 - s), 8)
        product(h, d)

        @pl.when(k >= 2)
        def _():
            rs_wait(way, k - 2)
            add(way, k - 2)

        def peak(i, carry):
            at = pl.ds(aligned(i * CHUNK, CHUNK), CHUNK)
            return jnp.maximum(carry, jnp.max(jnp.abs(acc[at, :]).reshape(CHUNK // 8, 8, WIDE), axis=0))

        top = lax.fori_loop(0, Q // CHUNK, peak, jnp.zeros((8, WIDE), jnp.float32))
        top = jnp.maximum(jnp.max(top, axis=0, keepdims=True) * 1.01, 1e-30).astype(jnp.bfloat16)
        scale = TOP / top.astype(jnp.float32)
        rs_send[way, k, Q : Q + 16, :] = jnp.broadcast_to(top.astype(jnp.float32), (16, WIDE)).astype(jnp.bfloat16)

        def rows(i, carry):
            at = pl.ds(aligned(i * CHUNK, CHUNK), CHUNK)
            rs_send[way, k, at, :] = encode(acc[at, :], scale)
            return carry

        lax.fori_loop(0, Q // CHUNK, rows, 0)
        rs_copy(way, k, 0).start()
        pl.when(mine4)(rs_copy(way, k, 1).start)

    def hg_copy(r, i):
        cols, width = ((BASE, 3 * LANES), (EXTRA, LANES))[i]
        dst = hg_out.at[:, pl.ds(aligned(my_first + i * 3 * LANES, LANES), width)]
        src = stage_h.at[pl.ds(aligned(r * T, 32), T), cols]
        return src, dst, remote(src, dst, g_s.at[r, i], g_r.at[i], partner(r)[1])

    def hg_piece(r):
        jj, _ = partner(r)
        rows = pl.ds(aligned(jj * T, 32), T)
        total = None
        for yh in (0, 1):
            for cc in (0, 1):
                part = jnp.dot(
                    og[yh, cc, rows, :], w[yh, pl.ds(cc * G, G), :], preferred_element_type=jnp.float32
                )
                total = part if total is None else total + part
        stage_h[pl.ds(aligned(r * T, 32), T), :] = total.astype(jnp.bfloat16)

        @pl.when(r == 0)
        def _():
            for i in (0, 1):
                src, dst, _ = hg_copy(0, i)
                local(src, dst, g_r.at[i], mine4 if i else None)

        @pl.when(r != 0)
        def _():
            hg_copy(r, 0)[2].start()
            pl.when(mine4)(hg_copy(r, 1)[2].start)

    def rs_pair(k, carry):
        rs_one(k, 0)
        rs_one(k, 1)

        @pl.when((k >= 1) & (k <= 4))
        def _():
            @pl.when(k == 1)
            def _():
                for h in (0, 1):
                    z_wait(4, h, h)

            def pieces(i, carry):
                hg_piece((k - 1) * 2 + i)
                return carry

            lax.fori_loop(0, 2, pieces, 0)

        return carry

    lax.fori_loop(0, 7, rs_pair, 0)

    for dy in (1, 0):
        h = lax.rem(y_lo + dy, 2)
        product(h, z)
        rs_wait(0, 6 - h)
        add(0, 6 - h)
        rs_wait(1, 5 + h)
        add(1, 5 + h)
        stage_w[dy] = acc[...]
        for dx in (2, 1, 3, 0):
            r = dy * 4 + dx
            xx = lax.rem(x + dx, 4)
            dev = partner(r)[1]
            for i, (cols, width) in enumerate(((BASE, 3 * LANES), (EXTRA, LANES))):
                src = stage_w.at[dy, pl.ds(aligned(xx * F, F), F), cols]
                dst = wg_out.at[:, pl.ds(aligned(my_first + i * 3 * LANES, LANES), width)]
                if r == 0:
                    local(src, dst, o_r.at[i], mine4 if i else None)
                else:
                    send(src, dst, o_s.at[r, i], o_r.at[i], dev, mine4 if i else None)

    for cond, copy in pending:
        if cond is None:
            copy.wait_send()
        else:
            pl.when(cond)(copy.wait_send)

    def hg_sent(r, carry):
        hg_copy(r, 0)[2].wait_send()
        pl.when(mine4)(hg_copy(r, 1)[2].wait_send)
        return carry

    lax.fori_loop(1, 8, hg_sent, 0)

    def rs_sent(i, carry):
        way, k = lax.rem(i, 2), lax.div(i, 2)
        rs_copy(way, k, 0).wait_send()
        pl.when(mine4)(rs_copy(way, k, 1).wait_send)
        return carry

    lax.fori_loop(0, 14, rs_sent, 0)
    for out, sem in ((hg_out, g_r), (wg_out, o_r)):
        arrived(out.at[:, pl.ds(0, 24 * LANES)], sem.at[0])
        arrived(out.at[:, pl.ds(0, 4 * LANES)], sem.at[1])


def shards(hidden, out_grad, weight):
    anywhere = pl.BlockSpec(memory_space=pl.ANY)
    dma = pltpu.SemaphoreType.DMA
    return pl.pallas_call(
        kernel,
        out_shape=(
            jax.ShapeDtypeStruct(hidden.shape, jnp.bfloat16),
            jax.ShapeDtypeStruct(weight.shape, jnp.float32),
        ),
        in_specs=[anywhere] * 3,
        out_specs=(anywhere, anywhere),
        scratch_shapes=[
            pltpu.VMEM((2, 2, 8 * T, G), jnp.bfloat16),
            pltpu.VMEM((2, 2 * G, WIDE), jnp.bfloat16),
            pltpu.VMEM((8 * T, WIDE), jnp.bfloat16),
            pltpu.VMEM((2, 7, Q + 16, WIDE), jnp.bfloat16),
            pltpu.VMEM((2, 7, Q + 16, WIDE), jnp.bfloat16),
            pltpu.VMEM((Q, WIDE), jnp.float32),
            pltpu.VMEM((8 * T, WIDE), jnp.bfloat16),
            pltpu.VMEM((2, Q, WIDE), jnp.float32),
            dma((1,)),
            dma((8, 2)), dma((2, 2)),
            dma((8, 2)), dma((2,)),
            dma((8, 2)), dma((2,)),
            dma((8, 2)), dma((2,)),
            dma((4,)), dma((4,)),
            dma((4, 4)), dma((4, 4)),
            dma((16,)), dma((1,)),
            dma((2, 4, 2, 2)), dma((2, 4, 2, 2)),
            dma((2, 7, 2)), dma((2, 7, 2)),
        ],
        compiler_params=pltpu.CompilerParams(
            collective_id=0, has_side_effects=True, vmem_limit_bytes=48 * 1024 * 1024
        ),
    )(hidden, out_grad, weight)


def solution(mesh):
    return jax.shard_map(
        shards,
        mesh=mesh,
        in_specs=(P("dp", "tensor"), P("dp", "tensor"), P("dp", "tensor")),
        out_specs=(P("dp", "tensor"), P("dp", "tensor")),
        check_vma=False,
    )
```

time: 1040 us -> 115 us (0.11)
  waiting for transfers between devices: 992 us -> 0 us
  Pallas kernels: 0 us -> 109 us
  matrix products: 37.3 us -> 0 us
  between operations: 13.8 us -> 0.65 us
    reduce_scatter x1 -> x0, waiting for transfers between devices: 654 us -> none  [shards(): lax.psum_scatter(lax.dot_general(columns, hidden, (((0,), (0,)), ((), ())...]
    all_gather x2 -> x0, waiting for transfers between devices: 336 us -> none  [the longest x1 306 us: shards(): lax.all_gather(weight, 'dp', axis=0, tiled=True)]
    pallas_call x0 -> x1, Pallas kernels: none -> 109 us  [shards(): pl.pallas_call(kernel, out_shape=(jax.ShapeDtypeStruct(hidden.shape, jnp....]
    dot_general x2 -> x0, matrix products: 37.3 us -> none  [the longest x1 24.2 us: shards(): lax.dot_general(columns, hidden, (((0,), (0,)), ((), ())), preferred_elem...]
  transfers between devices with their start and end apart: 3 -> 0, of which waited for: 3 -> 0; matrix products, arithmetic and copies ran while one was open for 4% -> 0% of each run, Pallas kernels for 0% -> 0%
where the time goes in v1:
time: 115 us; the launch traced here: 114 us
  Pallas kernels  109 us (95%)
  local copies, waits for them, and re-layouts  5.17 us (4%)
    pallas_call x1, Pallas kernels, shards(): pl.pallas_call(kernel, out_shape=(jax.ShapeDtypeStruct(hidden.shape, jnp....  109 us
    unnamed x8, local copies, waits for them, and re-layouts  5.17 us

profile of v1, /device:TPU:1, one launch (start us, length us, event | category | flops | bytes accessed | tf_op | source)
XLA Modules:
  0.0 114.3 jit_solution(5718838002395588043)
XLA Ops:
  0.6 0.0 copy-start
  0.6 1.2 %copy-done = bf16[160,3584]{1,0:T(8,128)(2,1)S(1)} copy-done((bf16[160,3584]{1,0:T(8,128)(2,1)S(1)}, bf16[160,3584]{1,0:T(8,128)(2,1)}, u32[]{:S(2)}) %copy-start) | copy-done | bytes 1146904
  1.9 0.0 copy-start.1
  1.9 1.0 copy-done.1
  2.9 0.0 copy-start.2
  2.9 1.0 copy-done.2
  3.9 108.5 %shard_map.50 = (bf16[160,3584]{1,0:T(8,128)(2,1)S(1)}, f32[64,3584]{1,0:T(8,128)S(1)}) custom-call(bf16[160,3584]{1,0:T(8,128)(2,1)S(1)} %copy-done, bf16[160,1024]{1,0:T(8,128)(2,1)S(1)} %copy-done.2, bf16[64,3584]{1,0:T(8,128)(2,1)S(1)} %copy-done.1), custom_call_target="tpu_custom_call" | custom-call | tf_op jit(solution)/shard_map/pallas_call | solution.py:386
  112.4 1.0 copy.7
  113.4 0.9 copy.8
Async XLA Ops:
  0.6 1.3 %copy-start = (bf16[160,3584]{1,0:T(8,128)(2,1)S(1)}, bf16[160,3584]{1,0:T(8,128)(2,1)}, u32[]{:S(2)}) copy-start(bf16[160,3584]{1,0:T(8,128)(2,1)} %hidden.1) | copy-start | bytes 3440644
  1.9 1.0 copy-start.1
  2.9 1.0 copy-start.2

commit v2 on v1

v2 whole, which is shorter than its diff:
```python
import jax
import jax.numpy as jnp
from jax import lax
from jax.experimental import pallas as pl
from jax.experimental.pallas import tpu as pltpu
from jax.sharding import PartitionSpec as P

MESH = pl.DeviceIdType.MESH
LANES = 128
BASE = pl.ds(0, 3 * LANES)
EXTRA = pl.ds(3 * LANES, LANES)
WIDE = 4 * LANES
T = 160
F = 64
G = 1024
Q = 256
CHUNK = 32
TOP = 32768.0
ORDERS = (
    (3, 2, 1, 0), (3, 2, 1, 0), (2, 1, 3, 0), (1, 0, 2, 3),
    (0, 1, 2, 3), (0, 1, 2, 3), (0, 1, 3, 2), (3, 0, 2, 1),
)


def aligned(value, step):
    return pl.multiple_of(value, step)


def encode(total, scale):
    t = total * scale
    t2 = t * t
    t4 = t2 * t2
    t8 = t4 * t4
    return jnp.where(t < 0, -t8, t8).astype(jnp.bfloat16)


def decode(code, scale):
    y = code.astype(jnp.float32)
    root = lax.rsqrt(lax.rsqrt(jnp.maximum(jnp.abs(y), 1e-37)))
    root = root * lax.rsqrt(root)
    return jnp.where(y < 0, -root, root) * scale


def kernel(
    hidden, grad, weight, hg_out, wg_out,
    og, w, hid, rs_send, rs_recv, acc, stage_h, stage_w,
    loc, w_s, w_r, h_s, h_r, g_s, g_r, o_s, o_r,
    a_s, a_r, b_s, b_r, s_s, s_r, y_s, z_s, z_r, r_s, r_r,
):
    dp, tensor = lax.axis_index("dp"), lax.axis_index("tensor")
    x, z, y_lo = lax.rem(dp, 4), lax.rem(lax.div(dp, 4), 8), lax.div(dp, 32)
    y_hi, core = lax.div(tensor, 2), lax.rem(tensor, 2)
    y, j = y_hi * 2 + y_lo, y_lo * 4 + x

    def device(xx, yy, zz, cc):
        return ((lax.rem(yy, 2) * 8 + zz) * 4 + xx, lax.div(yy, 2) * 2 + cc)

    def four(jj):
        return lax.rem(jj + core, 2) == 0

    def first(jj):
        return lax.div(7 * jj + 1 - core, 2) * LANES

    def partner(r):
        xx, yl = lax.rem(x + lax.rem(r, 4), 4), lax.rem(y_lo + lax.div(r, 4), 2)
        return yl * 4 + xx, device(xx, y_hi * 2 + yl, z, core)

    mine4 = four(j)
    my_first = first(j)
    sibling = device(x, y, z, 1 - core)

    barrier = pltpu.get_barrier_semaphore()
    greeted = [partner(r)[1] for r in range(1, 8)]
    greeted += [device(x, y, lax.rem(z + 1, 8), core), device(x, y, lax.rem(z + 7, 8), core)]
    greeted += [sibling, device(x, 3 - y, z, core)]
    for dev in greeted:
        pl.semaphore_signal(barrier, inc=1, device_id=dev, device_id_type=MESH)
    pl.semaphore_wait(barrier, len(greeted))

    pending = []

    def remote(src, dst, ss, rs, dev):
        return pltpu.make_async_remote_copy(
            src_ref=src, dst_ref=dst, send_sem=ss, recv_sem=rs, device_id=dev, device_id_type=MESH
        )

    def send(src, dst, ss, rs, dev, cond=None):
        copy = remote(src, dst, ss, rs, dev)
        if cond is None:
            copy.start()
        else:
            pl.when(cond)(copy.start)
        pending.append((cond, copy))

    def arrived(ref, sem, cond=None):
        copy = pltpu.make_async_copy(ref, ref, sem)
        if cond is None:
            copy.wait()
        else:
            pl.when(cond)(copy.wait)

    def local(src, dst, sem, cond=None):
        copy = pltpu.make_async_copy(src, dst, sem)
        if cond is None:
            copy.start()
        else:
            pl.when(cond)(copy.start)

    z_next = (device(x, y, lax.rem(z + 1, 8), core), device(x, y, lax.rem(z + 7, 8), core))
    halves = (y_lo, 1 - y_lo)

    def piece(xx):
        return pl.ds(aligned(z * Q + lax.rem(xx + 4, 4) * F, F), F)

    def z_rows(plane):
        return pl.ds(aligned(lax.rem(plane + 8, 8) * Q, Q), Q)

    def z_piece(r):
        h, rows = halves[r // 4], piece(x - r % 4)
        for i, cols in enumerate((BASE, EXTRA)):
            dst = w.at[h, rows, cols]
            src = dst
            if r == 0:
                src = weight.at[:, pl.ds(aligned(my_first + i * 3 * LANES, LANES), (3 - 2 * i) * LANES)]
            for way in (0, 1):
                send(src, dst, y_s.at[way, r, i], z_r.at[way, 0, r // 4, i], z_next[way], mine4 if i else None)

    def w_wait(r):
        h, rows = halves[r // 4], piece(x - r % 4)
        arrived(w.at[h, rows, BASE], w_r.at[r, 0])
        arrived(w.at[h, rows, EXTRA], w_r.at[r, 1], mine4)

    def z_wait(s, way, n):
        plane = z - s if way == 0 else z + s
        arrived(w.at[halves[n], z_rows(plane), BASE], z_r.at[way, s - 1, n, 0])
        arrived(w.at[halves[n], z_rows(plane), EXTRA], z_r.at[way, s - 1, n, 1], mine4)

    def z_step(s, n):
        for way in (0, 1):
            z_wait(s, way, n)
            if s == 3 and way != n:
                continue
            plane = z - s if way == 0 else z + s
            for i, cols in enumerate((BASE, EXTRA)):
                ref = w.at[halves[n], z_rows(plane), cols]
                send(ref, ref, z_s.at[way, s, n, i], z_r.at[way, s, n, i], z_next[way], mine4 if i else None)

    for r in (1, 3, 2, 4, 5, 7, 6):
        jj, dev = partner(r)
        c = aligned(first(jj), LANES)
        rows = piece(x)
        send(weight.at[:, pl.ds(c, 3 * LANES)], w.at[y_lo, rows, BASE], w_s.at[r, 0], w_r.at[r, 0], dev)
        send(
            weight.at[:, pl.ds(c + 3 * LANES, LANES)], w.at[y_lo, rows, EXTRA],
            w_s.at[r, 1], w_r.at[r, 1], dev, four(jj),
        )
    z_piece(0)

    a, b = x * (1 - core) + y * core, x * core + y * (1 - core)
    turn = lax.rem(4 * core - z + 8, 8)
    code = 0
    for e, order in enumerate(ORDERS):
        code = code + jnp.where(turn == e, sum(q * 4**p for p, q in enumerate(order)), 0)

    def place(aa, bb):
        aa, bb = lax.rem(aa, 4), lax.rem(bb, 4)
        return aa * (1 - core) + bb * core, aa * core + bb * (1 - core)

    def columns(p):
        return pl.ds(aligned(lax.rem(lax.div(code, 4**p), 4) * Q, Q), Q)

    def block(p, da, db, half=None):
        xx, yy = place(a + da, b + db)
        row = (lax.rem(yy, 2) * 4 + xx) * T
        rows = pl.ds(aligned(row, 32), T) if half is None else pl.ds(aligned(row + half * (T // 2), 16), T // 2)
        return og.at[lax.div(yy, 2), core, rows, columns(p)]

    def towards(da, db):
        xx, yy = place(a + da, b + db)
        return device(xx, yy, z, core)

    def og_start(p):
        src = grad.at[:, columns(p)]
        send(src, block(p, 0, 0), a_s.at[p, 0], a_r.at[p, 0], towards(1, 0))
        send(src, block(p, 0, 0), a_s.at[p, 1], a_r.at[p, 1], towards(3, 0))

    def og_line(p):
        arrived(block(p, 3, 0), a_r.at[p, 0])
        send(block(p, 3, 0, 0), block(p, 3, 0, 0), a_s.at[p, 2], a_r.at[p, 2], towards(1, 0))
        arrived(block(p, 1, 0), a_r.at[p, 1])
        send(block(p, 1, 0, 1), block(p, 1, 0, 1), a_s.at[p, 3], a_r.at[p, 3], towards(3, 0))
        for n, to in enumerate((towards(0, 1), towards(0, 3))):
            for da in (0, 3, 1):
                src = grad.at[:, columns(p)] if da == 0 else block(p, da, 0)
                send(src, block(p, da, 0), b_s.at[p, da, n], b_r.at[p, n], to)
        arrived(block(p, 2, 0, 0), a_r.at[p, 2])
        arrived(block(p, 2, 0, 1), a_r.at[p, 3])
        for n, to in enumerate((towards(0, 1), towards(0, 3))):
            send(block(p, 2, 0), block(p, 2, 0), b_s.at[p, 2, n], b_r.at[p, n], to)

    def og_plane(p):
        for n, (db, to) in enumerate(((3, towards(0, 1)), (1, towards(0, 3)))):
            arrived(og.at[0, 0, pl.ds(0, 4 * T), pl.ds(0, Q)], b_r.at[p, n])
            for da in range(4):
                ref = block(p, da, db, n)
                send(ref, ref, b_s.at[p, da, 2 + n], b_r.at[p, 2 + n], to)

    def og_share(p):
        for n in (2, 3):
            arrived(og.at[0, 0, pl.ds(0, 2 * T), pl.ds(0, Q)], b_r.at[p, n])
        if p == 0:
            arrived(grad, loc.at[0])
        ref = og.at[:, core, :, columns(p)]
        send(ref, ref, s_s.at[p], s_r.at[p], sibling)

    def og_wait(p):
        arrived(og.at[:, core, :, pl.ds(0, Q)], s_r.at[p])

    og_start(0)
    xx, yy = place(a, b)
    local(grad, og.at[lax.div(yy, 2), core, pl.ds(aligned((lax.rem(yy, 2) * 4 + xx) * T, 32), T), :], loc.at[0])

    h_rows = pl.ds(aligned(j * T, 32), T)
    for r in (2, 6, 1, 3, 5, 7, 4):
        jj, dev = partner(r)
        c = aligned(first(jj), LANES)
        send(hidden.at[:, pl.ds(c, 3 * LANES)], hid.at[h_rows, BASE], h_s.at[r, 0], h_r.at[0], dev)
        send(
            hidden.at[:, pl.ds(c + 3 * LANES, LANES)], hid.at[h_rows, EXTRA],
            h_s.at[r, 1], h_r.at[1], dev, four(jj),
        )
    for p in (1, 2, 3):
        og_start(p)
    c = aligned(my_first, LANES)
    local(weight.at[:, pl.ds(c, 3 * LANES)], w.at[y_lo, piece(x), BASE], w_r.at[0, 0])
    local(weight.at[:, pl.ds(c + 3 * LANES, LANES)], w.at[y_lo, piece(x), EXTRA], w_r.at[0, 1], mine4)
    local(hidden.at[:, pl.ds(c, 3 * LANES)], hid.at[h_rows, BASE], h_r.at[0])
    local(hidden.at[:, pl.ds(c + 3 * LANES, LANES)], hid.at[h_rows, EXTRA], h_r.at[1], mine4)

    for r in (1, 3, 2, 4, 5, 7, 6):
        w_wait(r)
        z_piece(r)
    w_wait(0)
    og_line(0)
    z_step(1, 0)
    og_line(1)
    z_step(1, 1)
    og_plane(0)
    z_step(2, 0)
    og_share(0)
    og_line(2)
    og_plane(1)
    z_step(2, 1)
    og_share(1)
    og_line(3)
    og_plane(2)
    z_step(3, 0)
    og_share(2)
    og_plane(3)
    z_step(3, 1)

    def product(h, d, lo, n):
        lhs = og[h, lax.div(d, 4), :, pl.ds(aligned(lax.rem(d, 4) * Q + lo, LANES), n)]
        acc[0:n, :] = lax.dot_general(lhs, hid[...], (((0,), (0,)), ((), ())), preferred_element_type=jnp.float32)

    def add(way, k, src, dst, n):
        scale = rs_recv[way, k, Q : Q + 16, :].astype(jnp.float32)[0:1, :] * (1.0 / TOP)

        def rows(i, carry):
            at = pl.ds(aligned(dst + i * CHUNK, CHUNK), CHUNK)
            acc[at, :] += decode(rs_recv[way, k, pl.ds(aligned(src + i * CHUNK, CHUNK), CHUNK), :], scale)
            return carry

        lax.fori_loop(0, n, rows, 0)

    def put(way, k, src, dst, n):
        def peak(i, carry):
            at = pl.ds(aligned(i * CHUNK, CHUNK), CHUNK)
            return jnp.maximum(carry, jnp.max(jnp.abs(acc[at, :]).reshape(CHUNK // 8, 8, WIDE), axis=0))

        top = lax.fori_loop(0, n, peak, jnp.zeros((8, WIDE), jnp.float32))
        top = jnp.maximum(jnp.max(top, axis=0, keepdims=True) * 1.01, 1e-30).astype(jnp.bfloat16)
        scale = TOP / top.astype(jnp.float32)
        rs_send[way, k, Q : Q + 16, :] = jnp.broadcast_to(top.astype(jnp.float32), (16, WIDE)).astype(jnp.bfloat16)

        def rows(i, carry):
            at = pl.ds(aligned(i * CHUNK, CHUNK), CHUNK)
            rs_send[way, k, pl.ds(aligned(dst + i * CHUNK, CHUNK), CHUNK), :] = encode(acc[at, :], scale)
            return carry

        lax.fori_loop(0, n, rows, 0)

    def rs_rows(small):
        return pl.ds(Q // 2, Q // 2 + 16) if small else pl.ds(0, Q + 16)

    def rs_wait(way, k, small):
        arrived(rs_recv.at[way, k, rs_rows(small), BASE], r_r.at[way, k, 0])
        arrived(rs_recv.at[way, k, rs_rows(small), EXTRA], r_r.at[way, k, 1], mine4)

    def rs_copy(way, k, i, small):
        cols = (BASE, EXTRA)[i]
        to = device(x, y, lax.rem(z + 1 + 6 * way, 8), core)
        return remote(
            rs_send.at[way, k, rs_rows(small), cols], rs_recv.at[way, k, rs_rows(small), cols],
            r_s.at[way, k, i], r_r.at[way, k, i], to,
        )

    def half_of(n):
        return n * y_lo + (1 - n) * (1 - y_lo)

    def rs_first(i, carry):
        n, way = lax.div(i, 2), lax.rem(i, 2)
        product(half_of(n), lax.rem(z + 4, 8), way * (Q // 2), Q // 2)
        put(way, n, 0, Q // 2, Q // 2 // CHUNK)
        rs_copy(way, n, 0, True).start()
        pl.when(mine4)(rs_copy(way, n, 1, True).start)
        return carry

    def rs_next(small):
        def one(i, carry):
            k, way = lax.div(i, 2), lax.rem(i, 2)
            s = lax.div(k, 2) + 1
            product(half_of(lax.rem(k, 2)), lax.rem(z + 8 + (1 - 2 * way) * (5 - s), 8), 0, Q)
            rs_wait(way, k - 2, small)
            if small:
                add(way, k - 2, Q // 2, way * (Q // 2), Q // 2 // CHUNK)
            else:
                add(way, k - 2, 0, 0, Q // CHUNK)
            put(way, k, 0, 0, Q // CHUNK)
            rs_copy(way, k, 0, False).start()
            pl.when(mine4)(rs_copy(way, k, 1, False).start)
            return carry

        return one

    def hg_copy(r, i):
        cols, width = ((BASE, 3 * LANES), (EXTRA, LANES))[i]
        dst = hg_out.at[:, pl.ds(aligned(my_first + i * 3 * LANES, LANES), width)]
        src = stage_h.at[pl.ds(aligned(r * T, 32), T), cols]
        return src, dst, remote(src, dst, g_s.at[r, i], g_r.at[i], partner(r)[1])

    def hg_piece(r, carry):
        jj, _ = partner(r)
        rows = pl.ds(aligned(jj * T, 32), T)
        total = None
        for yh in (0, 1):
            for cc in (0, 1):
                part = jnp.dot(
                    og[yh, cc, rows, :], w[yh, pl.ds(cc * G, G), :], preferred_element_type=jnp.float32
                )
                total = part if total is None else total + part
        stage_h[pl.ds(aligned(r * T, 32), T), :] = total.astype(jnp.bfloat16)

        @pl.when(r == 0)
        def _():
            for i in (0, 1):
                src, dst, _ = hg_copy(0, i)
                local(src, dst, g_r.at[i], mine4 if i else None)

        @pl.when(r != 0)
        def _():
            hg_copy(r, 0)[2].start()
            pl.when(mine4)(hg_copy(r, 1)[2].start)

        return carry

    og_wait(0)
    arrived(hid.at[:, BASE], h_r.at[0])
    arrived(hid.at[:, EXTRA], h_r.at[1], mine4)
    lax.fori_loop(0, 4, rs_first, 0)
    og_share(3)
    og_wait(1)
    og_wait(2)
    lax.fori_loop(4, 8, rs_next(True), 0)
    for n in (0, 1):
        z_wait(4, n, n)
    og_wait(3)
    lax.fori_loop(0, 8, hg_piece, 0)
    lax.fori_loop(8, 16, rs_next(False), 0)

    for n in (0, 1):
        product(half_of(n), z, 0, Q)
        for way in (0, 1):
            rs_wait(way, 6 + n, False)
            add(way, 6 + n, 0, 0, Q // CHUNK)
        stage_w[n] = acc[...]
        for dx in (2, 1, 3, 0):
            r = (1 - n) * 4 + dx
            xx = lax.rem(x + dx, 4)
            dev = partner(r)[1]
            for i, (cols, width) in enumerate(((BASE, 3 * LANES), (EXTRA, LANES))):
                src = stage_w.at[n, pl.ds(aligned(xx * F, F), F), cols]
                dst = wg_out.at[:, pl.ds(aligned(my_first + i * 3 * LANES, LANES), width)]
                if r == 0:
                    local(src, dst, o_r.at[i], mine4 if i else None)
                else:
                    send(src, dst, o_s.at[r, i], o_r.at[i], dev, mine4 if i else None)
        if n == 0:
            late = len(pending)
            for cond, copy in pending[: late - 8]:
                if cond is None:
                    copy.wait_send()
                else:
                    pl.when(cond)(copy.wait_send)

    for cond, copy in pending[late - 8 :]:
        if cond is None:
            copy.wait_send()
        else:
            pl.when(cond)(copy.wait_send)

    def hg_sent(r, carry):
        hg_copy(r, 0)[2].wait_send()
        pl.when(mine4)(hg_copy(r, 1)[2].wait_send)
        return carry

    lax.fori_loop(1, 8, hg_sent, 0)

    def rs_sent(small):
        def one(i, carry):
            k, way = lax.div(i, 2), lax.rem(i, 2)
            rs_copy(way, k, 0, small).wait_send()
            pl.when(mine4)(rs_copy(way, k, 1, small).wait_send)
            return carry

        return one

    lax.fori_loop(0, 4, rs_sent(True), 0)
    lax.fori_loop(4, 16, rs_sent(False), 0)
    for out, sem in ((hg_out, g_r), (wg_out, o_r)):
        arrived(out.at[:, pl.ds(0, 24 * LANES)], sem.at[0])
        arrived(out.at[:, pl.ds(0, 4 * LANES)], sem.at[1])


def shards(hidden, out_grad, weight):
    anywhere = pl.BlockSpec(memory_space=pl.ANY)
    dma = pltpu.SemaphoreType.DMA
    return pl.pallas_call(
        kernel,
        out_shape=(
            jax.ShapeDtypeStruct(hidden.shape, jnp.bfloat16),
            jax.ShapeDtypeStruct(weight.shape, jnp.float32),
        ),
        in_specs=[anywhere] * 3,
        out_specs=(anywhere, anywhere),
        scratch_shapes=[
            pltpu.VMEM((2, 2, 8 * T, G), jnp.bfloat16),
            pltpu.VMEM((2, 2 * G, WIDE), jnp.bfloat16),
            pltpu.VMEM((8 * T, WIDE), jnp.bfloat16),
            pltpu.VMEM((2, 8, Q + 16, WIDE), jnp.bfloat16),
            pltpu.VMEM((2, 8, Q + 16, WIDE), jnp.bfloat16),
            pltpu.VMEM((Q, WIDE), jnp.float32),
            pltpu.VMEM((8 * T, WIDE), jnp.bfloat16),
            pltpu.VMEM((2, Q, WIDE), jnp.float32),
            dma((1,)),
            dma((8, 2)), dma((8, 2)),
            dma((8, 2)), dma((2,)),
            dma((8, 2)), dma((2,)),
            dma((8, 2)), dma((2,)),
            dma((4, 4)), dma((4, 4)),
            dma((4, 4, 4)), dma((4, 4)),
            dma((4,)), dma((4,)),
            dma((2, 8, 2)),
            dma((2, 4, 2, 2)), dma((2, 4, 2, 2)),
            dma((2, 8, 2)), dma((2, 8, 2)),
        ],
        compiler_params=pltpu.CompilerParams(
            collective_id=0, has_side_effects=True, vmem_limit_bytes=63 * 1024 * 1024
        ),
    )(hidden, out_grad, weight)


def solution(mesh):
    return jax.shard_map(
        shards,
        mesh=mesh,
        in_specs=(P("dp", "tensor"), P("dp", "tensor"), P("dp", "tensor")),
        out_specs=(P("dp", "tensor"), P("dp", "tensor")),
        check_vma=False,
    )
```

time: 115 us -> 122 us (1.061)
  Pallas kernels: 109 us -> 118 us
  local copies, waits for them, and re-layouts: 5.17 us -> 3.34 us
    pallas_call x1, Pallas kernels: 109 us -> 118 us  [shards(): pl.pallas_call(kernel, out_shape=(jax.ShapeDtypeStruct(hidden.shape, jnp....]
    unnamed x8 -> x4, local copies, waits for them, and re-layouts: 5.17 us -> 3.34 us
where the time goes in v2:
time: 122 us
  Pallas kernels  118 us (97%)
  local copies, waits for them, and re-layouts  3.34 us (3%)
    pallas_call x1, Pallas kernels, shards(): pl.pallas_call(kernel, out_shape=(jax.ShapeDtypeStruct(hidden.shape, jnp....  118 us
    unnamed x4, local copies, waits for them, and re-layouts  3.34 us

profile of v2, /device:TPU:1, one launch (start us, length us, event | category | flops | bytes accessed | tf_op | source)
XLA Modules:
  0.0 122.0 jit_solution(9293377350624005813)
XLA Ops:
  0.6 118.0 %shard_map.50 = (bf16[160,3584]{1,0:T(8,128)(2,1)}, f32[64,3584]{1,0:T(8,128)}) custom-call(bf16[160,3584]{1,0:T(8,128)(2,1)} %hidden.1, bf16[160,1024]{1,0:T(8,128)(2,1)} %grad.1, bf16[64,3584]{1,0:T(8,128)(2,1)} %weight.1), custom_call_target="tpu_custom_call" | custom-call | tf_op jit(solution)/shard_map/pallas_call | solution.py:438
  118.7 0.0 copy-start
  118.7 2.4 %copy.7 = bf16[160,3584]{1,0:T(8,128)(2,1)} copy(bf16[160,3584]{1,0:T(8,128)(2,1)} %get-tuple-element.4) | data formatting | bytes 2293760
  121.1 0.0 copy-done
  121.1 0.9 copy.8
Async XLA Ops:
  118.7 2.4 %copy-start = (f32[64,3584]{1,0:T(8,128)S(1)}, f32[64,3584]{1,0:T(8,128)}, u32[]{:S(2)}) copy-start(f32[64,3584]{1,0:T(8,128)} %get-tuple-element.5) | copy-start | bytes 2752516

commit v3 on v2

--- a/solution.py
+++ b/solution.py
@@ -12,10 +12,15 @@
 WIDE = 4 * LANES
 T = 160
 F = 64
-G = 1024
 Q = 256
 CHUNK = 32
 TOP = 32768.0
+SCHEDULE = (
+    ("start", 0), ("start", 1), ("start", 2), ("start", 3), ("pieces",), ("line", 0), ("z", 0, 1), ("line", 1), ("z", 1, 0),
+    ("line", 2), ("line", 3), ("z", 1, 1), ("opposite", 0), ("opposite", 1), ("z", 2, 0), ("opposite", 2), ("opposite", 3),
+    ("hidden",), ("z", 2, 1), ("plane", 0), ("plane", 1), ("plane", 2), ("plane", 3), ("z", 3, 0), ("z", 3, 1), ("last", 0),
+    ("first",), ("last", 1), ("last", 2), ("second",), ("last", 3),
+)
 ORDERS = (
     (3, 2, 1, 0), (3, 2, 1, 0), (2, 1, 3, 0), (1, 0, 2, 3),
     (0, 1, 2, 3), (0, 1, 2, 3), (0, 1, 3, 2), (3, 0, 2, 1),
@@ -116,14 +121,14 @@
         return pl.ds(aligned(lax.rem(plane + 8, 8) * Q, Q), Q)
 
     def z_piece(r):
-        h, rows = halves[r // 4], piece(x - r % 4)
+        rows = piece(x - r)
         for i, cols in enumerate((BASE, EXTRA)):
-            dst = w.at[h, rows, cols]
+            dst = w.at[y_lo, rows, cols]
             src = dst
             if r == 0:
                 src = weight.at[:, pl.ds(aligned(my_first + i * 3 * LANES, LANES), (3 - 2 * i) * LANES)]
             for way in (0, 1):
-                send(src, dst, y_s.at[way, r, i], z_r.at[way, 0, r // 4, i], z_next[way], mine4 if i else None)
+                send(src, dst, y_s.at[way, r, i], z_r.at[way, 0, 0, i], z_next[way], mine4 if i else None)
 
     def w_wait(r):
         h, rows = halves[r // 4], piece(x - r % 4)
@@ -136,8 +141,12 @@
         arrived(w.at[halves[n], z_rows(plane), EXTRA], z_r.at[way, s - 1, n, 1], mine4)
 
     def z_step(s, n):
+        if s == 0:
+            for r in (4, 5, 7, 6):
+                w_wait(r)
         for way in (0, 1):
-            z_wait(s, way, n)
+            if s:
+                z_wait(s, way, n)
             if s == 3 and way != n:
                 continue
             plane = z - s if way == 0 else z + s
@@ -162,106 +171,103 @@
     for e, order in enumerate(ORDERS):
         code = code + jnp.where(turn == e, sum(q * 4**p for p, q in enumerate(order)), 0)
 
-    def place(aa, bb):
-        aa, bb = lax.rem(aa, 4), lax.rem(bb, 4)
-        return aa * (1 - core) + bb * core, aa * core + bb * (1 - core)
-
-    def columns(p):
-        return pl.ds(aligned(lax.rem(lax.div(code, 4**p), 4) * Q, Q), Q)
-
-    def block(p, da, db, half=None):
-        xx, yy = place(a + da, b + db)
-        row = (lax.rem(yy, 2) * 4 + xx) * T
-        rows = pl.ds(aligned(row, 32), T) if half is None else pl.ds(aligned(row + half * (T // 2), 16), T // 2)
-        return og.at[lax.div(yy, 2), core, rows, columns(p)]
-
     def towards(da, db):
-        xx, yy = place(a + da, b + db)
-        return device(xx, yy, z, core)
+        aa, bb = lax.rem(a + da, 4), lax.rem(b + db, 4)
+        return device(aa * (1 - core) + bb * core, aa * core + bb * (1 - core), z, core)
+
+    to_a, to_b = (towards(1, 0), towards(3, 0)), (towards(0, 1), towards(0, 3))
+    quarters = [lax.rem(lax.div(code, 4**p), 4) for p in range(4)]
+    a_at, b_at = [lax.rem(a + n, 4) for n in range(4)], [lax.rem(b + n, 4) for n in range(4)]
+    mine = [grad.at[:, pl.ds(aligned(q * Q, Q), Q)] for q in quarters]
+
+    def block(p, da, half=None):
+        ref = og.at[core, quarters[p], b, a_at[da]]
+        return ref if half is None else ref.at[pl.ds(half * (T // 2), T // 2), :]
+
+    def line(p, db, half=None):
+        ref = og.at[core, quarters[p], b_at[db]]
+        return ref if half is None else ref.at[pl.ds(2 * half, 2)]
 
     def og_start(p):
-        src = grad.at[:, columns(p)]
-        send(src, block(p, 0, 0), a_s.at[p, 0], a_r.at[p, 0], towards(1, 0))
-        send(src, block(p, 0, 0), a_s.at[p, 1], a_r.at[p, 1], towards(3, 0))
+        for n in (0, 1):
+            send(mine[p], block(p, 0), a_s.at[p, n], a_r.at[p, n], to_a[n])
+        for n in (0, 1):
+            send(mine[p], block(p, 0), b_s.at[p, 0, n], b_r.at[p, n], to_b[n])
+        local(mine[p], block(p, 0), loc.at[p])
+
+    def og_share(p, db):
+        ref = line(p, db)
+        send(ref, ref, s_s.at[p, db], s_r.at[p], sibling)
 
     def og_line(p):
-        arrived(block(p, 3, 0), a_r.at[p, 0])
-        send(block(p, 3, 0, 0), block(p, 3, 0, 0), a_s.at[p, 2], a_r.at[p, 2], towards(1, 0))
-        arrived(block(p, 1, 0), a_r.at[p, 1])
-        send(block(p, 1, 0, 1), block(p, 1, 0, 1), a_s.at[p, 3], a_r.at[p, 3], towards(3, 0))
-        for n, to in enumerate((towards(0, 1), towards(0, 3))):
-            for da in (0, 3, 1):
-                src = grad.at[:, columns(p)] if da == 0 else block(p, da, 0)
-                send(src, block(p, da, 0), b_s.at[p, da, n], b_r.at[p, n], to)
-        arrived(block(p, 2, 0, 0), a_r.at[p, 2])
-        arrived(block(p, 2, 0, 1), a_r.at[p, 3])
-        for n, to in enumerate((towards(0, 1), towards(0, 3))):
-            send(block(p, 2, 0), block(p, 2, 0), b_s.at[p, 2, n], b_r.at[p, n], to)
+        for n, da in enumerate((3, 1)):
+            arrived(block(p, da), a_r.at[p, n])
+            send(block(p, da, n), block(p, da, n), a_s.at[p, 2 + n], a_r.at[p, 2 + n], to_a[n])
+            for m in (0, 1):
+                send(block(p, da), block(p, da), b_s.at[p, da, m], b_r.at[p, m], to_b[m])
+
+    def og_opposite(p):
+        for n in (0, 1):
+            arrived(block(p, 2, n), a_r.at[p, 2 + n])
+        for n in (0, 1):
+            send(block(p, 2), block(p, 2), b_s.at[p, 2, n], b_r.at[p, n], to_b[n])
+        arrived(block(p, 0), loc.at[p])
+        og_share(p, 0)
 
     def og_plane(p):
-        for n, (db, to) in enumerate(((3, towards(0, 1)), (1, towards(0, 3)))):
-            arrived(og.at[0, 0, pl.ds(0, 4 * T), pl.ds(0, Q)], b_r.at[p, n])
-            for da in range(4):
-                ref = block(p, da, db, n)
-                send(ref, ref, b_s.at[p, da, 2 + n], b_r.at[p, 2 + n], to)
-
-    def og_share(p):
-        for n in (2, 3):
-            arrived(og.at[0, 0, pl.ds(0, 2 * T), pl.ds(0, Q)], b_r.at[p, n])
-        if p == 0:
-            arrived(grad, loc.at[0])
-        ref = og.at[:, core, :, columns(p)]
-        send(ref, ref, s_s.at[p], s_r.at[p], sibling)
+        for n, db in enumerate((3, 1)):
+            arrived(line(p, db), b_r.at[p, n])
+            send(line(p, db, n), line(p, db, n), b_s.at[p, 4, n], b_r.at[p, 2 + n], to_b[n])
+            og_share(p, db)
+
+    def og_last(p):
+        for n in (0, 1):
+            arrived(line(p, 2, n), b_r.at[p, 2 + n])
+        og_share(p, 2)
 
     def og_wait(p):
-        arrived(og.at[:, core, :, pl.ds(0, Q)], s_r.at[p])
-
-    og_start(0)
-    xx, yy = place(a, b)
-    local(grad, og.at[lax.div(yy, 2), core, pl.ds(aligned((lax.rem(yy, 2) * 4 + xx) * T, 32), T), :], loc.at[0])
-
-    h_rows = pl.ds(aligned(j * T, 32), T)
-    for r in (2, 6, 1, 3, 5, 7, 4):
-        jj, dev = partner(r)
-        c = aligned(first(jj), LANES)
-        send(hidden.at[:, pl.ds(c, 3 * LANES)], hid.at[h_rows, BASE], h_s.at[r, 0], h_r.at[0], dev)
-        send(
-            hidden.at[:, pl.ds(c + 3 * LANES, LANES)], hid.at[h_rows, EXTRA],
-            h_s.at[r, 1], h_r.at[1], dev, four(jj),
-        )
-    for p in (1, 2, 3):
-        og_start(p)
+        arrived(og.at[core, 0], s_r.at[p])
+
+
+    def hidden_start():
+        h_block = hid.at[y_lo, x]
+        for r in (2, 6, 1, 3, 5, 7, 4):
+            jj, dev = partner(r)
+            c = aligned(first(jj), LANES)
+            send(hidden.at[:, pl.ds(c, 3 * LANES)], h_block.at[:, BASE], h_s.at[r, 0], h_r.at[0], dev)
+            send(
+                hidden.at[:, pl.ds(c + 3 * LANES, LANES)], h_block.at[:, EXTRA],
+                h_s.at[r, 1], h_r.at[1], dev, four(jj),
+            )
+        c = aligned(my_first, LANES)
+        local(hidden.at[:, pl.ds(c, 3 * LANES)], h_block.at[:, BASE], h_r.at[0])
+        local(hidden.at[:, pl.ds(c + 3 * LANES, LANES)], h_block.at[:, EXTRA], h_r.at[1], mine4)
+
     c = aligned(my_first, LANES)
     local(weight.at[:, pl.ds(c, 3 * LANES)], w.at[y_lo, piece(x), BASE], w_r.at[0, 0])
     local(weight.at[:, pl.ds(c + 3 * LANES, LANES)], w.at[y_lo, piece(x), EXTRA], w_r.at[0, 1], mine4)
-    local(hidden.at[:, pl.ds(c, 3 * LANES)], hid.at[h_rows, BASE], h_r.at[0])
-    local(hidden.at[:, pl.ds(c + 3 * LANES, LANES)], hid.at[h_rows, EXTRA], h_r.at[1], mine4)
-
-    for r in (1, 3, 2, 4, 5, 7, 6):
-        w_wait(r)
-        z_piece(r)
-    w_wait(0)
-    og_line(0)
-    z_step(1, 0)
-    og_line(1)
-    z_step(1, 1)
-    og_plane(0)
-    z_step(2, 0)
-    og_share(0)
-    og_line(2)
-    og_plane(1)
-    z_step(2, 1)
-    og_share(1)
-    og_line(3)
-    og_plane(2)
-    z_step(3, 0)
-    og_share(2)
-    og_plane(3)
-    z_step(3, 1)
+
+    def pieces():
+        for r in (1, 3, 2):
+            w_wait(r)
+            z_piece(r)
 
     def product(h, d, lo, n):
-        lhs = og[h, lax.div(d, 4), :, pl.ds(aligned(lax.rem(d, 4) * Q + lo, LANES), n)]
-        acc[0:n, :] = lax.dot_general(lhs, hid[...], (((0,), (0,)), ((), ())), preferred_element_type=jnp.float32)
+        q, cols = lax.rem(d, 4), pl.ds(aligned(lo, LANES), n)
+        contract = (((0,), (0,)), ((), ()))
+
+        @pl.when(d < 4)
+        def _():
+            lhs = og[0, q, pl.ds(2 * h, 2), :, :, cols].reshape(8 * T, n)
+            acc[0:n, :] = lax.dot_general(
+                lhs, hid[...].reshape(8 * T, WIDE), contract, preferred_element_type=jnp.float32
+            )
+
+        @pl.when(d >= 4)
+        def _():
+            lhs = og[1, q, :, pl.ds(2 * h, 2), :, cols].reshape(8 * T, n)
+            rhs = jnp.concatenate([hid[i % 2, i // 2] for i in range(8)], axis=0)
+            acc[0:n, :] = lax.dot_general(lhs, rhs, contract, preferred_element_type=jnp.float32)
 
     def add(way, k, src, dst, n):
         scale = rs_recv[way, k, Q : Q + 16, :].astype(jnp.float32)[0:1, :] * (1.0 / TOP)
@@ -273,19 +279,19 @@
 
         lax.fori_loop(0, n, rows, 0)
 
-    def put(way, k, src, dst, n):
+    def pack(src, to, dst, n, tail):
         def peak(i, carry):
-            at = pl.ds(aligned(i * CHUNK, CHUNK), CHUNK)
+            at = pl.ds(aligned(src + i * CHUNK, CHUNK), CHUNK)
             return jnp.maximum(carry, jnp.max(jnp.abs(acc[at, :]).reshape(CHUNK // 8, 8, WIDE), axis=0))
 
         top = lax.fori_loop(0, n, peak, jnp.zeros((8, WIDE), jnp.float32))
         top = jnp.maximum(jnp.max(top, axis=0, keepdims=True) * 1.01, 1e-30).astype(jnp.bfloat16)
         scale = TOP / top.astype(jnp.float32)
-        rs_send[way, k, Q : Q + 16, :] = jnp.broadcast_to(top.astype(jnp.float32), (16, WIDE)).astype(jnp.bfloat16)
+        to[tail : tail + 16, :] = jnp.broadcast_to(top.astype(jnp.float32), (16, WIDE)).astype(jnp.bfloat16)
 
         def rows(i, carry):
-            at = pl.ds(aligned(i * CHUNK, CHUNK), CHUNK)
-            rs_send[way, k, pl.ds(aligned(dst + i * CHUNK, CHUNK), CHUNK), :] = encode(acc[at, :], scale)
+            at = pl.ds(aligned(src + i * CHUNK, CHUNK), CHUNK)
+            to[pl.ds(aligned(dst + i * CHUNK, CHUNK), CHUNK), :] = encode(acc[at, :], scale)
             return carry
 
         lax.fori_loop(0, n, rows, 0)
@@ -311,7 +317,7 @@
     def rs_first(i, carry):
         n, way = lax.div(i, 2), lax.rem(i, 2)
         product(half_of(n), lax.rem(z + 4, 8), way * (Q // 2), Q // 2)
-        put(way, n, 0, Q // 2, Q // 2 // CHUNK)
+        pack(0, rs_send.at[way, n], Q // 2, Q // 2 // CHUNK, Q)
         rs_copy(way, n, 0, True).start()
         pl.when(mine4)(rs_copy(way, n, 1, True).start)
         return carry
@@ -326,7 +332,7 @@
                 add(way, k - 2, Q // 2, way * (Q // 2), Q // 2 // CHUNK)
             else:
                 add(way, k - 2, 0, 0, Q // CHUNK)
-            put(way, k, 0, 0, Q // CHUNK)
+            pack(0, rs_send.at[way, k], 0, Q // CHUNK, Q)
             rs_copy(way, k, 0, False).start()
             pl.when(mine4)(rs_copy(way, k, 1, False).start)
             return carry
@@ -340,14 +346,12 @@
         return src, dst, remote(src, dst, g_s.at[r, i], g_r.at[i], partner(r)[1])
 
     def hg_piece(r, carry):
-        jj, _ = partner(r)
-        rows = pl.ds(aligned(jj * T, 32), T)
+        xx, yl = lax.rem(x + lax.rem(r, 4), 4), lax.rem(y_lo + lax.div(r, 4), 2)
         total = None
         for yh in (0, 1):
-            for cc in (0, 1):
-                part = jnp.dot(
-                    og[yh, cc, rows, :], w[yh, pl.ds(cc * G, G), :], preferred_element_type=jnp.float32
-                )
+            for q in range(8):
+                lhs = og[0, q, 2 * yh + yl, xx] if q < 4 else og[1, q - 4, xx, 2 * yh + yl]
+                part = jnp.dot(lhs, w[yh, pl.ds(q * Q, Q), :], preferred_element_type=jnp.float32)
                 total = part if total is None else total + part
         stage_h[pl.ds(aligned(r * T, 32), T), :] = total.astype(jnp.bfloat16)
 
@@ -364,16 +368,25 @@
 
         return carry
 
-    og_wait(0)
-    arrived(hid.at[:, BASE], h_r.at[0])
-    arrived(hid.at[:, EXTRA], h_r.at[1], mine4)
-    lax.fori_loop(0, 4, rs_first, 0)
-    og_share(3)
-    og_wait(1)
-    og_wait(2)
-    lax.fori_loop(4, 8, rs_next(True), 0)
+    def sums_first():
+        og_wait(0)
+        arrived(hid.at[:, :, :, BASE], h_r.at[0])
+        arrived(hid.at[:, :, :, EXTRA], h_r.at[1], mine4)
+        lax.fori_loop(0, 4, rs_first, 0)
+
+    def sums_second():
+        og_wait(1)
+        og_wait(2)
+        lax.fori_loop(4, 8, rs_next(True), 0)
+
+    steps = {"z": z_step, "line": og_line, "opposite": og_opposite, "plane": og_plane, "last": og_last, "first": sums_first, "second": sums_second,
+             "start": og_start, "hidden": hidden_start, "pieces": pieces}
+    for name, *numbers in SCHEDULE:
+        steps[name](*numbers)
+
     for n in (0, 1):
         z_wait(4, n, n)
+    w_wait(0)
     og_wait(3)
     lax.fori_loop(0, 8, hg_piece, 0)
     lax.fori_loop(8, 16, rs_next(False), 0)
@@ -383,13 +396,14 @@
         for way in (0, 1):
             rs_wait(way, 6 + n, False)
             add(way, 6 + n, 0, 0, Q // CHUNK)
-        stage_w[n] = acc[...]
+        for xx in range(4):
+            pack(xx * F, stage_w.at[n, xx], 0, F // CHUNK, F)
         for dx in (2, 1, 3, 0):
             r = (1 - n) * 4 + dx
             xx = lax.rem(x + dx, 4)
             dev = partner(r)[1]
             for i, (cols, width) in enumerate(((BASE, 3 * LANES), (EXTRA, LANES))):
-                src = stage_w.at[n, pl.ds(aligned(xx * F, F), F), cols]
+                src = stage_w.at[n, xx, :, cols]
                 dst = wg_out.at[:, pl.ds(aligned(my_first + i * 3 * LANES, LANES), width)]
                 if r == 0:
                     local(src, dst, o_r.at[i], mine4 if i else None)
@@ -432,35 +446,61 @@
         arrived(out.at[:, pl.ds(0, 4 * LANES)], sem.at[1])
 
 
+def finish(hg, code, hg_out, wg_out, held, total, rows, come, go, into, out_of):
+    part = held.shape[1] // 4
+    parts = [pl.ds(i * part, part) for i in range(4)]
+    copies = [pltpu.make_async_copy(code.at[:, at], held.at[:, at], come.at[i]) for i, at in enumerate(parts)]
+    for copy in copies:
+        copy.start()
+    shares = [pl.ds(i * (T // 5), T // 5) for i in range(5)]
+    ins = [pltpu.make_async_copy(hg.at[at], rows.at[at], into.at[i]) for i, at in enumerate(shares)]
+    outs = [pltpu.make_async_copy(rows.at[at], hg_out.at[at], out_of.at[i]) for i, at in enumerate(shares)]
+    for copy in ins:
+        copy.start()
+    back = [pltpu.make_async_copy(total.at[:, at], wg_out.at[:, at], go.at[i]) for i, at in enumerate(parts)]
+    for copy, out, at in zip(copies, back, parts):
+        copy.wait()
+        scale = held[F : F + 16, at].astype(jnp.float32)[0:1, :] * (1.0 / TOP)
+        for row in range(0, F, 16):
+            total[row : row + 16, at] = decode(held[row : row + 16, at], scale)
+        out.start()
+        if at is parts[0]:
+            for arrive, leave in zip(ins, outs):
+                arrive.wait()
+                leave.start()
+    for copy in outs + back:
+        copy.wait()
+
+
 def shards(hidden, out_grad, weight):
     anywhere = pl.BlockSpec(memory_space=pl.ANY)
     dma = pltpu.SemaphoreType.DMA
-    return pl.pallas_call(
+    hidden_grad, code = pl.pallas_call(
         kernel,
         out_shape=(
             jax.ShapeDtypeStruct(hidden.shape, jnp.bfloat16),
-            jax.ShapeDtypeStruct(weight.shape, jnp.float32),
+            jax.ShapeDtypeStruct((F + 16, weight.shape[1]), jnp.bfloat16),
         ),
         in_specs=[anywhere] * 3,
         out_specs=(anywhere, anywhere),
         scratch_shapes=[
-            pltpu.VMEM((2, 2, 8 * T, G), jnp.bfloat16),
-            pltpu.VMEM((2, 2 * G, WIDE), jnp.bfloat16),
-            pltpu.VMEM((8 * T, WIDE), jnp.bfloat16),
+            pltpu.VMEM((2, 4, 4, 4, T, Q), jnp.bfloat16),
+            pltpu.VMEM((2, 8 * Q, WIDE), jnp.bfloat16),
+            pltpu.VMEM((2, 4, T, WIDE), jnp.bfloat16),
             pltpu.VMEM((2, 8, Q + 16, WIDE), jnp.bfloat16),
             pltpu.VMEM((2, 8, Q + 16, WIDE), jnp.bfloat16),
             pltpu.VMEM((Q, WIDE), jnp.float32),
             pltpu.VMEM((8 * T, WIDE), jnp.bfloat16),
-            pltpu.VMEM((2, Q, WIDE), jnp.float32),
-            dma((1,)),
+            pltpu.VMEM((2, 4, F + 16, WIDE), jnp.bfloat16),
+            dma((4,)),
             dma((8, 2)), dma((8, 2)),
             dma((8, 2)), dma((2,)),
             dma((8, 2)), dma((2,)),
             dma((8, 2)), dma((2,)),
             dma((4, 4)), dma((4, 4)),
-            dma((4, 4, 4)), dma((4, 4)),
-            dma((4,)), dma((4,)),
-            dma((2, 8, 2)),
+            dma((4, 5, 2)), dma((4, 4)),
+            dma((4, 4)), dma((4,)),
+            dma((2, 4, 2)),
             dma((2, 4, 2, 2)), dma((2, 4, 2, 2)),
             dma((2, 8, 2)), dma((2, 8, 2)),
         ],
@@ -468,6 +508,22 @@
             collective_id=0, has_side_effects=True, vmem_limit_bytes=63 * 1024 * 1024
         ),
     )(hidden, out_grad, weight)
+    return pl.pallas_call(
+        finish,
+        out_shape=(
+            jax.ShapeDtypeStruct(hidden.shape, jnp.bfloat16),
+            jax.ShapeDtypeStruct(weight.shape, jnp.float32),
+        ),
+        in_specs=[anywhere] * 2,
+        out_specs=(anywhere, anywhere),
+        scratch_shapes=[
+            pltpu.VMEM((F + 16, weight.shape[1]), jnp.bfloat16),
+            pltpu.VMEM(weight.shape, jnp.float32),
+            pltpu.VMEM(hidden.shape, jnp.bfloat16),
+            dma((4,)), dma((4,)), dma((5,)), dma((5,)),
+        ],
+        compiler_params=pltpu.CompilerParams(vmem_limit_bytes=63 * 1024 * 1024),
+    )(hidden_grad, code)
 
 
 def solution(mesh):

time: 122 us -> 106 us (0.87)
  Pallas kernels: 118 us -> 104 us
  local copies, waits for them, and re-layouts: 3.34 us -> 0 us
    pallas_call x1, Pallas kernels: 118 us -> 102 us  [shards(): pl.pallas_call(kernel, out_shape=(jax.ShapeDtypeStruct(hidden.shape, jnp....]
    unnamed x4 -> x0, local copies, waits for them, and re-layouts: 3.34 us -> none
    pallas_call x0 -> x1, Pallas kernels: none -> 2.7 us  [shards(): pl.pallas_call(finish, out_shape=(jax.ShapeDtypeStruct(hidden.shape, jnp....]
where the time goes in v3:
time: 106 us; the launch traced here: 105 us
  Pallas kernels  104 us (98%)
    pallas_call x1, Pallas kernels, shards(): pl.pallas_call(kernel, out_shape=(jax.ShapeDtypeStruct(hidden.shape, jnp....  102 us
    pallas_call x1, Pallas kernels, shards(): pl.pallas_call(finish, out_shape=(jax.ShapeDtypeStruct(hidden.shape, jnp....  2.7 us

profile of v3, /device:TPU:1, one launch (start us, length us, event | category | flops | bytes accessed | tf_op | source)
XLA Modules:
  0.0 104.9 jit_solution(10923636895630120859)
XLA Ops:
  0.6 101.6 %shard_map.50 = (bf16[160,3584]{1,0:T(8,128)(2,1)}, bf16[80,3584]{1,0:T(8,128)(2,1)}) custom-call(bf16[160,3584]{1,0:T(8,128)(2,1)} %hidden.1, bf16[160,1024]{1,0:T(8,128)(2,1)} %grad.1, bf16[64,3584]{1,0:T(8,128)(2,1)} %weight.1), custom_call_target="tpu_custom_call" | custom-call | tf_op jit(solution)/shard_map/pallas_call | solution.py:478
  102.2 2.7 %shard_map.51 = (bf16[160,3584]{1,0:T(8,128)(2,1)}, f32[64,3584]{1,0:T(8,128)}) custom-call(bf16[160,3584]{1,0:T(8,128)(2,1)} %get-tuple-element.4.hg, bf16[80,3584]{1,0:T(8,128)(2,1)} %get-tuple-element.5.code), custom_call_target="tpu_custom_call" | custom-call | tf_op jit(solution)/shard_map/pallas_call | solution.py:511

commit v4 on v3

--- a/solution.py
+++ b/solution.py
@@ -13,13 +13,14 @@
 T = 160
 F = 64
 Q = 256
+S = 128
 CHUNK = 32
 TOP = 32768.0
 SCHEDULE = (
     ("start", 0), ("start", 1), ("start", 2), ("start", 3), ("pieces",), ("line", 0), ("z", 0, 1), ("line", 1), ("z", 1, 0),
-    ("line", 2), ("line", 3), ("z", 1, 1), ("opposite", 0), ("opposite", 1), ("z", 2, 0), ("opposite", 2), ("opposite", 3),
-    ("hidden",), ("z", 2, 1), ("plane", 0), ("plane", 1), ("plane", 2), ("plane", 3), ("z", 3, 0), ("z", 3, 1), ("last", 0),
-    ("first",), ("last", 1), ("last", 2), ("second",), ("last", 3),
+    ("line", 2), ("z", 1, 1), ("opposite", 0), ("opposite", 1), ("opposite", 2), ("hidden",), ("z", 2, 0), ("plane", 0),
+    ("plane", 1), ("plane", 2), ("line", 3), ("z", 2, 1), ("opposite", 3), ("z", 3, 0), ("z", 3, 1), ("last", 0),
+    ("first",), ("last", 1), ("last", 2), ("plane", 3), ("second",), ("last", 3),
 )
 ORDERS = (
     (3, 2, 1, 0), (3, 2, 1, 0), (2, 1, 3, 0), (1, 0, 2, 3),
@@ -154,6 +155,7 @@
                 ref = w.at[halves[n], z_rows(plane), cols]
                 send(ref, ref, z_s.at[way, s, n, i], z_r.at[way, s, n, i], z_next[way], mine4 if i else None)
 
+    z_piece(0)
     for r in (1, 3, 2, 4, 5, 7, 6):
         jj, dev = partner(r)
         c = aligned(first(jj), LANES)
@@ -163,7 +165,6 @@
             weight.at[:, pl.ds(c + 3 * LANES, LANES)], w.at[y_lo, rows, EXTRA],
             w_s.at[r, 1], w_r.at[r, 1], dev, four(jj),
         )
-    z_piece(0)
 
     a, b = x * (1 - core) + y * core, x * core + y * (1 - core)
     turn = lax.rem(4 * core - z + 8, 8)
@@ -252,92 +253,121 @@
             w_wait(r)
             z_piece(r)
 
-    def product(h, d, lo, n):
-        q, cols = lax.rem(d, 4), pl.ds(aligned(lo, LANES), n)
+    def product(h, d, r):
+        q, cols = lax.rem(d, 4), pl.ds(aligned(r * S, S), S)
         contract = (((0,), (0,)), ((), ()))
 
         @pl.when(d < 4)
         def _():
-            lhs = og[0, q, pl.ds(2 * h, 2), :, :, cols].reshape(8 * T, n)
-            acc[0:n, :] = lax.dot_general(
+            lhs = og[0, q, pl.ds(2 * h, 2), :, :, cols].reshape(8 * T, S)
+            acc[...] = lax.dot_general(
                 lhs, hid[...].reshape(8 * T, WIDE), contract, preferred_element_type=jnp.float32
             )
 
         @pl.when(d >= 4)
         def _():
-            lhs = og[1, q, :, pl.ds(2 * h, 2), :, cols].reshape(8 * T, n)
+            lhs = og[1, q, :, pl.ds(2 * h, 2), :, cols].reshape(8 * T, S)
             rhs = jnp.concatenate([hid[i % 2, i // 2] for i in range(8)], axis=0)
-            acc[0:n, :] = lax.dot_general(lhs, rhs, contract, preferred_element_type=jnp.float32)
-
-    def add(way, k, src, dst, n):
-        scale = rs_recv[way, k, Q : Q + 16, :].astype(jnp.float32)[0:1, :] * (1.0 / TOP)
+            acc[...] = lax.dot_general(lhs, rhs, contract, preferred_element_type=jnp.float32)
+
+    def at_tile(t, i):
+        return pl.ds(aligned(16 + t * S + i * CHUNK, 16), CHUNK), pl.ds(t * LANES, LANES)
+
+    def add(way, m):
+        peaks = rs_recv[way, m, 0:16, :].astype(jnp.float32) * (1.0 / TOP)
 
         def rows(i, carry):
-            at = pl.ds(aligned(dst + i * CHUNK, CHUNK), CHUNK)
-            acc[at, :] += decode(rs_recv[way, k, pl.ds(aligned(src + i * CHUNK, CHUNK), CHUNK), :], scale)
+            at = pl.ds(aligned(i * CHUNK, CHUNK), CHUNK)
+            for t in range(4):
+                held, cols = at_tile(t, i)
+                acc[at, cols] += decode(rs_recv[way, m, held, :], peaks[t : t + 1, :])
             return carry
 
-        lax.fori_loop(0, n, rows, 0)
-
-    def pack(src, to, dst, n, tail):
+        lax.fori_loop(0, S // CHUNK, rows, 0)
+
+    def peak_of(src, n):
         def peak(i, carry):
             at = pl.ds(aligned(src + i * CHUNK, CHUNK), CHUNK)
             return jnp.maximum(carry, jnp.max(jnp.abs(acc[at, :]).reshape(CHUNK // 8, 8, WIDE), axis=0))
 
         top = lax.fori_loop(0, n, peak, jnp.zeros((8, WIDE), jnp.float32))
-        top = jnp.maximum(jnp.max(top, axis=0, keepdims=True) * 1.01, 1e-30).astype(jnp.bfloat16)
-        scale = TOP / top.astype(jnp.float32)
-        to[tail : tail + 16, :] = jnp.broadcast_to(top.astype(jnp.float32), (16, WIDE)).astype(jnp.bfloat16)
+        top = jnp.maximum(jnp.max(top, axis=0, keepdims=True) * 1.01, 1e-30)
+        return top.astype(jnp.bfloat16).astype(jnp.float32)
+
+    def pack_ring(way, m):
+        top = peak_of(0, S // CHUNK)
+        scale = TOP / top
+        row = lax.broadcasted_iota(jnp.int32, (16, LANES), 0)
+        peaks = jnp.broadcast_to(top[:, 0:LANES], (16, LANES))
+        for t in range(1, 4):
+            peaks = jnp.where(row == t, jnp.broadcast_to(top[:, t * LANES : (t + 1) * LANES], (16, LANES)), peaks)
+        rs_send[way, m, 0:16, :] = peaks.astype(jnp.bfloat16)
 
         def rows(i, carry):
-            at = pl.ds(aligned(src + i * CHUNK, CHUNK), CHUNK)
-            to[pl.ds(aligned(dst + i * CHUNK, CHUNK), CHUNK), :] = encode(acc[at, :], scale)
+            at = pl.ds(aligned(i * CHUNK, CHUNK), CHUNK)
+            for t in range(4):
+                held, cols = at_tile(t, i)
+                rs_send[way, m, held, :] = encode(acc[at, cols], scale[:, t * LANES : (t + 1) * LANES])
             return carry
 
-        lax.fori_loop(0, n, rows, 0)
-
-    def rs_rows(small):
-        return pl.ds(Q // 2, Q // 2 + 16) if small else pl.ds(0, Q + 16)
-
-    def rs_wait(way, k, small):
-        arrived(rs_recv.at[way, k, rs_rows(small), BASE], r_r.at[way, k, 0])
-        arrived(rs_recv.at[way, k, rs_rows(small), EXTRA], r_r.at[way, k, 1], mine4)
-
-    def rs_copy(way, k, i, small):
-        cols = (BASE, EXTRA)[i]
+        lax.fori_loop(0, S // CHUNK, rows, 0)
+
+    def pack_out(src, to):
+        top = peak_of(src, F // CHUNK)
+        scale = TOP / top
+        to[F : F + 16, :] = jnp.broadcast_to(top, (16, WIDE)).astype(jnp.bfloat16)
+        for i in range(F // CHUNK):
+            to[i * CHUNK : (i + 1) * CHUNK, :] = encode(acc[src + i * CHUNK : src + (i + 1) * CHUNK, :], scale)
+
+    rs_parts = (pl.ds(0, 16 + 3 * S), pl.ds(16 + 3 * S, S))
+
+    def rs_wait(way, m):
+        arrived(rs_recv.at[way, m, rs_parts[0]], r_r.at[way, m, 0])
+        arrived(rs_recv.at[way, m, rs_parts[1]], r_r.at[way, m, 1], mine4)
+
+    def rs_copy(way, m, i):
         to = device(x, y, lax.rem(z + 1 + 6 * way, 8), core)
         return remote(
-            rs_send.at[way, k, rs_rows(small), cols], rs_recv.at[way, k, rs_rows(small), cols],
-            r_s.at[way, k, i], r_r.at[way, k, i], to,
+            rs_send.at[way, m, rs_parts[i]], rs_recv.at[way, m, rs_parts[i]], r_s.at[way, m, i], r_r.at[way, m, i], to
         )
+
+    def rs_put(way, m):
+        pack_ring(way, m)
+        rs_copy(way, m, 0).start()
+        pl.when(mine4)(rs_copy(way, m, 1).start)
 
     def half_of(n):
         return n * y_lo + (1 - n) * (1 - y_lo)
 
     def rs_first(i, carry):
-        n, way = lax.div(i, 2), lax.rem(i, 2)
-        product(half_of(n), lax.rem(z + 4, 8), way * (Q // 2), Q // 2)
-        pack(0, rs_send.at[way, n], Q // 2, Q // 2 // CHUNK, Q)
-        rs_copy(way, n, 0, True).start()
-        pl.when(mine4)(rs_copy(way, n, 1, True).start)
-        return carry
-
-    def rs_next(small):
-        def one(i, carry):
-            k, way = lax.div(i, 2), lax.rem(i, 2)
-            s = lax.div(k, 2) + 1
-            product(half_of(lax.rem(k, 2)), lax.rem(z + 8 + (1 - 2 * way) * (5 - s), 8), 0, Q)
-            rs_wait(way, k - 2, small)
-            if small:
-                add(way, k - 2, Q // 2, way * (Q // 2), Q // 2 // CHUNK)
-            else:
-                add(way, k - 2, 0, 0, Q // CHUNK)
-            pack(0, rs_send.at[way, k], 0, Q // CHUNK, Q)
-            rs_copy(way, k, 0, False).start()
-            pl.when(mine4)(rs_copy(way, k, 1, False).start)
-            return carry
-
-        return one
+        m, way = lax.div(i, 2), lax.rem(i, 2)
+        product(half_of(m), lax.rem(z + 4, 8), way)
+        rs_put(way, m)
+        return carry
+
+    def rs_second(i, carry):
+        m, way = lax.div(i, 2), lax.rem(i, 2)
+        n, old = lax.div(m - 2, 2), lax.rem(m, 2)
+        product(half_of(n), lax.rem(z + 3 + 2 * way, 8), old * way + (1 - old) * (1 - way))
+
+        @pl.when(old == 1)
+        def _():
+            rs_wait(way, n)
+            add(way, n)
+
+        rs_put(way, m)
+        return carry
+
+    def rs_later(i, carry):
+        m, way = lax.div(i, 2), lax.rem(i, 2)
+        near, u = lax.div(m - 6, 4), lax.rem(m - 6, 4)
+        n, r = lax.div(u, 2), lax.rem(u, 2)
+        product(half_of(n), lax.rem(z + 8 + (1 - 2 * way) * (2 - near), 8), r)
+        before = jnp.where(near == 0, 2 + 2 * n + 1 - r - way + 2 * r * way, m - 4)
+        rs_wait(way, before)
+        add(way, before)
+        rs_put(way, m)
+        return carry
 
     def hg_copy(r, i):
         cols, width = ((BASE, 3 * LANES), (EXTRA, LANES))[i]
@@ -377,7 +407,7 @@
     def sums_second():
         og_wait(1)
         og_wait(2)
-        lax.fori_loop(4, 8, rs_next(True), 0)
+        lax.fori_loop(4, 12, rs_second, 0)
 
     steps = {"z": z_step, "line": og_line, "opposite": og_opposite, "plane": og_plane, "last": og_last, "first": sums_first, "second": sums_second,
              "start": og_start, "hidden": hidden_start, "pieces": pieces}
@@ -388,28 +418,32 @@
         z_wait(4, n, n)
     w_wait(0)
     og_wait(3)
-    lax.fori_loop(0, 8, hg_piece, 0)
-    lax.fori_loop(8, 16, rs_next(False), 0)
-
-    for n in (0, 1):
-        product(half_of(n), z, 0, Q)
+    lax.fori_loop(0, 4, hg_piece, 0)
+
+    def rs_rest(m, carry):
+        lax.fori_loop(2 * m, 2 * m + 2, rs_later, 0)
+        pl.when(m < 10)(lambda: hg_piece(m - 2, None))
+        return carry
+
+    lax.fori_loop(6, 14, rs_rest, 0)
+
+    for n, r in ((0, 0), (0, 1), (1, 0), (1, 1)):
+        product(half_of(n), z, r)
         for way in (0, 1):
-            rs_wait(way, 6 + n, False)
-            add(way, 6 + n, 0, 0, Q // CHUNK)
-        for xx in range(4):
-            pack(xx * F, stage_w.at[n, xx], 0, F // CHUNK, F)
-        for dx in (2, 1, 3, 0):
-            r = (1 - n) * 4 + dx
-            xx = lax.rem(x + dx, 4)
-            dev = partner(r)[1]
+            rs_wait(way, 10 + 2 * n + r)
+            add(way, 10 + 2 * n + r)
+        for xx in (2 * r, 2 * r + 1):
+            pack_out((xx - 2 * r) * F, stage_w.at[n, xx])
+            dev = device(xx, y_hi * 2 + half_of(n), z, core)
             for i, (cols, width) in enumerate(((BASE, 3 * LANES), (EXTRA, LANES))):
                 src = stage_w.at[n, xx, :, cols]
                 dst = wg_out.at[:, pl.ds(aligned(my_first + i * 3 * LANES, LANES), width)]
-                if r == 0:
-                    local(src, dst, o_r.at[i], mine4 if i else None)
+                if n == 0:
+                    send(src, dst, o_s.at[xx, i], o_r.at[i], dev, mine4 if i else None)
                 else:
-                    send(src, dst, o_s.at[r, i], o_r.at[i], dev, mine4 if i else None)
-        if n == 0:
+                    send(src, dst, o_s.at[4 + xx, i], o_r.at[i], dev, (x != xx) & mine4 if i else x != xx)
+                    local(src, dst, o_r.at[i], (x == xx) & mine4 if i else x == xx)
+        if (n, r) == (0, 1):
             late = len(pending)
             for cond, copy in pending[: late - 8]:
                 if cond is None:
@@ -430,17 +464,13 @@
 
     lax.fori_loop(1, 8, hg_sent, 0)
 
-    def rs_sent(small):
-        def one(i, carry):
-            k, way = lax.div(i, 2), lax.rem(i, 2)
-            rs_copy(way, k, 0, small).wait_send()
-            pl.when(mine4)(rs_copy(way, k, 1, small).wait_send)
-            return carry
-
-        return one
-
-    lax.fori_loop(0, 4, rs_sent(True), 0)
-    lax.fori_loop(4, 16, rs_sent(False), 0)
+    def rs_sent(i, carry):
+        m, way = lax.div(i, 2), lax.rem(i, 2)
+        rs_copy(way, m, 0).wait_send()
+        pl.when(mine4)(rs_copy(way, m, 1).wait_send)
+        return carry
+
+    lax.fori_loop(0, 28, rs_sent, 0)
     for out, sem in ((hg_out, g_r), (wg_out, o_r)):
         arrived(out.at[:, pl.ds(0, 24 * LANES)], sem.at[0])
         arrived(out.at[:, pl.ds(0, 4 * LANES)], sem.at[1])
@@ -487,9 +517,9 @@
             pltpu.VMEM((2, 4, 4, 4, T, Q), jnp.bfloat16),
             pltpu.VMEM((2, 8 * Q, WIDE), jnp.bfloat16),
             pltpu.VMEM((2, 4, T, WIDE), jnp.bfloat16),
-            pltpu.VMEM((2, 8, Q + 16, WIDE), jnp.bfloat16),
-            pltpu.VMEM((2, 8, Q + 16, WIDE), jnp.bfloat16),
-            pltpu.VMEM((Q, WIDE), jnp.float32),
+            pltpu.VMEM((2, 14, 16 + 4 * S, LANES), jnp.bfloat16),
+            pltpu.VMEM((2, 14, 16 + 4 * S, LANES), jnp.bfloat16),
+            pltpu.VMEM((S, WIDE), jnp.float32),
             pltpu.VMEM((8 * T, WIDE), jnp.bfloat16),
             pltpu.VMEM((2, 4, F + 16, WIDE), jnp.bfloat16),
             dma((4,)),
@@ -502,7 +532,7 @@
             dma((4, 4)), dma((4,)),
             dma((2, 4, 2)),
             dma((2, 4, 2, 2)), dma((2, 4, 2, 2)),
-            dma((2, 8, 2)), dma((2, 8, 2)),
+            dma((2, 14, 2)), dma((2, 14, 2)),
         ],
         compiler_params=pltpu.CompilerParams(
             collective_id=0, has_side_effects=True, vmem_limit_bytes=63 * 1024 * 1024

time: 106 us -> 99.2 us (0.936)
  Pallas kernels: 104 us -> 97.2 us
    pallas_call x1, Pallas kernels: 102 us -> 94.5 us  [shards(): pl.pallas_call(kernel, out_shape=(jax.ShapeDtypeStruct(hidden.shape, jnp....]
where the time goes in v4:
time: 99.2 us; the launch traced here: 97.8 us
  Pallas kernels  97.2 us (98%)
    pallas_call x1, Pallas kernels, shards(): pl.pallas_call(kernel, out_shape=(jax.ShapeDtypeStruct(hidden.shape, jnp....  94.5 us
    pallas_call x1, Pallas kernels, shards(): pl.pallas_call(finish, out_shape=(jax.ShapeDtypeStruct(hidden.shape, jnp....  2.7 us

profile of v4, /device:TPU:1, one launch (start us, length us, event | category | flops | bytes accessed | tf_op | source)
XLA Modules:
  0.0 97.8 jit_solution(2242009365589380071)
XLA Ops:
  0.6 94.5 %shard_map.50 = (bf16[160,3584]{1,0:T(8,128)(2,1)}, bf16[80,3584]{1,0:T(8,128)(2,1)}) custom-call(bf16[160,3584]{1,0:T(8,128)(2,1)} %hidden.1, bf16[160,1024]{1,0:T(8,128)(2,1)} %grad.1, bf16[64,3584]{1,0:T(8,128)(2,1)} %weight.1), custom_call_target="tpu_custom_call" | custom-call | tf_op jit(solution)/shard_map/pallas_call | solution.py:508
  95.1 2.7 %shard_map.51 = (bf16[160,3584]{1,0:T(8,128)(2,1)}, f32[64,3584]{1,0:T(8,128)}) custom-call(bf16[160,3584]{1,0:T(8,128)(2,1)} %get-tuple-element.4.hg, bf16[80,3584]{1,0:T(8,128)(2,1)} %get-tuple-element.5.code), custom_call_target="tpu_custom_call" | custom-call | tf_op jit(solution)/shard_map/pallas_call | solution.py:541

commit v5 on v4

--- a/solution.py
+++ b/solution.py
@@ -17,10 +17,10 @@
 CHUNK = 32
 TOP = 32768.0
 SCHEDULE = (
-    ("start", 0), ("start", 1), ("start", 2), ("start", 3), ("pieces",), ("line", 0), ("z", 0, 1), ("line", 1), ("z", 1, 0),
+    ("start", 0), ("pieces",), ("start", 1), ("start", 2), ("z", 0, 1), ("start", 3), ("line", 0), ("line", 1), ("z", 1, 0),
     ("line", 2), ("z", 1, 1), ("opposite", 0), ("opposite", 1), ("opposite", 2), ("hidden",), ("z", 2, 0), ("plane", 0),
-    ("plane", 1), ("plane", 2), ("line", 3), ("z", 2, 1), ("opposite", 3), ("z", 3, 0), ("z", 3, 1), ("last", 0),
-    ("first",), ("last", 1), ("last", 2), ("plane", 3), ("second",), ("last", 3),
+    ("plane", 1), ("plane", 2), ("line", 3), ("z", 2, 1), ("z", 3, 0), ("z", 3, 1), ("last", 0), ("opposite", 3),
+    ("first",), ("last", 1), ("last", 2), ("plane", 3), ("second", 0), ("second", 1), ("last", 3),
 )
 ORDERS = (
     (3, 2, 1, 0), (3, 2, 1, 0), (2, 1, 3, 0), (1, 0, 2, 3),
@@ -283,14 +283,14 @@
                 acc[at, cols] += decode(rs_recv[way, m, held, :], peaks[t : t + 1, :])
             return carry
 
-        lax.fori_loop(0, S // CHUNK, rows, 0)
+        lax.fori_loop(0, S // CHUNK, rows, 0, unroll=True)
 
     def peak_of(src, n):
         def peak(i, carry):
             at = pl.ds(aligned(src + i * CHUNK, CHUNK), CHUNK)
             return jnp.maximum(carry, jnp.max(jnp.abs(acc[at, :]).reshape(CHUNK // 8, 8, WIDE), axis=0))
 
-        top = lax.fori_loop(0, n, peak, jnp.zeros((8, WIDE), jnp.float32))
+        top = lax.fori_loop(0, n, peak, jnp.zeros((8, WIDE), jnp.float32), unroll=True)
         top = jnp.maximum(jnp.max(top, axis=0, keepdims=True) * 1.01, 1e-30)
         return top.astype(jnp.bfloat16).astype(jnp.float32)
 
@@ -310,7 +310,7 @@
                 rs_send[way, m, held, :] = encode(acc[at, cols], scale[:, t * LANES : (t + 1) * LANES])
             return carry
 
-        lax.fori_loop(0, S // CHUNK, rows, 0)
+        lax.fori_loop(0, S // CHUNK, rows, 0, unroll=True)
 
     def pack_out(src, to):
         top = peak_of(src, F // CHUNK)
@@ -404,10 +404,11 @@
         arrived(hid.at[:, :, :, EXTRA], h_r.at[1], mine4)
         lax.fori_loop(0, 4, rs_first, 0)
 
-    def sums_second():
-        og_wait(1)
-        og_wait(2)
-        lax.fori_loop(4, 12, rs_second, 0)
+    def sums_second(n):
+        if n == 0:
+            og_wait(1)
+            og_wait(2)
+        lax.fori_loop(4 + 4 * n, 8 + 4 * n, rs_second, 0)
 
     steps = {"z": z_step, "line": og_line, "opposite": og_opposite, "plane": og_plane, "last": og_last, "first": sums_first, "second": sums_second,
              "start": og_start, "hidden": hidden_start, "pieces": pieces}
@@ -420,9 +421,34 @@
     og_wait(3)
     lax.fori_loop(0, 4, hg_piece, 0)
 
+    def hg_sent(r, carry):
+        hg_copy(r, 0)[2].wait_send()
+        pl.when(mine4)(hg_copy(r, 1)[2].wait_send)
+        return carry
+
+    def rs_sent(i, carry):
+        m, way = lax.div(i, 2), lax.rem(i, 2)
+        rs_copy(way, m, 0).wait_send()
+        pl.when(mine4)(rs_copy(way, m, 1).wait_send)
+        return carry
+
+    def sent(copies):
+        for cond, copy in copies:
+            if cond is None:
+                copy.wait_send()
+            else:
+                pl.when(cond)(copy.wait_send)
+
+    early = list(pending)
+    pending.clear()
+
     def rs_rest(m, carry):
         lax.fori_loop(2 * m, 2 * m + 2, rs_later, 0)
         pl.when(m < 10)(lambda: hg_piece(m - 2, None))
+        rs_sent(2 * (m - 6), None)
+        rs_sent(2 * (m - 6) + 1, None)
+        for n in range(4):
+            pl.when(m == 10 + n)(lambda n=n: sent(early[n::4]))
         return carry
 
     lax.fori_loop(6, 14, rs_rest, 0)
@@ -444,33 +470,11 @@
                     send(src, dst, o_s.at[4 + xx, i], o_r.at[i], dev, (x != xx) & mine4 if i else x != xx)
                     local(src, dst, o_r.at[i], (x == xx) & mine4 if i else x == xx)
         if (n, r) == (0, 1):
-            late = len(pending)
-            for cond, copy in pending[: late - 8]:
-                if cond is None:
-                    copy.wait_send()
-                else:
-                    pl.when(cond)(copy.wait_send)
-
-    for cond, copy in pending[late - 8 :]:
-        if cond is None:
-            copy.wait_send()
-        else:
-            pl.when(cond)(copy.wait_send)
-
-    def hg_sent(r, carry):
-        hg_copy(r, 0)[2].wait_send()
-        pl.when(mine4)(hg_copy(r, 1)[2].wait_send)
-        return carry
-
-    lax.fori_loop(1, 8, hg_sent, 0)
-
-    def rs_sent(i, carry):
-        m, way = lax.div(i, 2), lax.rem(i, 2)
-        rs_copy(way, m, 0).wait_send()
-        pl.when(mine4)(rs_copy(way, m, 1).wait_send)
-        return carry
-
-    lax.fori_loop(0, 28, rs_sent, 0)
+            lax.fori_loop(1, 8, hg_sent, 0)
+            lax.fori_loop(16, 22, rs_sent, 0)
+
+    sent(pending)
+    lax.fori_loop(22, 28, rs_sent, 0)
     for out, sem in ((hg_out, g_r), (wg_out, o_r)):
         arrived(out.at[:, pl.ds(0, 24 * LANES)], sem.at[0])
         arrived(out.at[:, pl.ds(0, 4 * LANES)], sem.at[1])

time: 99.2 us -> 96.8 us (0.976)
  Pallas kernels: 97.2 us -> 95.6 us
    pallas_call x1, Pallas kernels: 94.5 us -> 92.9 us  [shards(): pl.pallas_call(kernel, out_shape=(jax.ShapeDtypeStruct(hidden.shape, jnp....]
where the time goes in v5:
time: 96.8 us; the launch traced here: 96.2 us
  Pallas kernels  95.6 us (99%)
    pallas_call x1, Pallas kernels, shards(): pl.pallas_call(kernel, out_shape=(jax.ShapeDtypeStruct(hidden.shape, jnp....  92.9 us
    pallas_call x1, Pallas kernels, shards(): pl.pallas_call(finish, out_shape=(jax.ShapeDtypeStruct(hidden.shape, jnp....  2.7 us

profile of v5, /device:TPU:1, one launch (start us, length us, event | category | flops | bytes accessed | tf_op | source)
XLA Modules:
  0.0 96.2 jit_solution(17179008388599659025)
XLA Ops:
  0.6 92.9 %shard_map.50 = (bf16[160,3584]{1,0:T(8,128)(2,1)}, bf16[80,3584]{1,0:T(8,128)(2,1)}) custom-call(bf16[160,3584]{1,0:T(8,128)(2,1)} %hidden.1, bf16[160,1024]{1,0:T(8,128)(2,1)} %grad.1, bf16[64,3584]{1,0:T(8,128)(2,1)} %weight.1), custom_call_target="tpu_custom_call" | custom-call | tf_op jit(solution)/shard_map/pallas_call | solution.py:512
  93.5 2.7 %shard_map.51 = (bf16[160,3584]{1,0:T(8,128)(2,1)}, f32[64,3584]{1,0:T(8,128)}) custom-call(bf16[160,3584]{1,0:T(8,128)(2,1)} %get-tuple-element.4.hg, bf16[80,3584]{1,0:T(8,128)(2,1)} %get-tuple-element.5.code), custom_call_target="tpu_custom_call" | custom-call | tf_op jit(solution)/shard_map/pallas_call | solution.py:545

commit v6 on v5

--- a/solution.py
+++ b/solution.py
@@ -492,16 +492,15 @@
     for copy in ins:
         copy.start()
     back = [pltpu.make_async_copy(total.at[:, at], wg_out.at[:, at], go.at[i]) for i, at in enumerate(parts)]
+    for arrive, leave in zip(ins, outs):
+        arrive.wait()
+        leave.start()
     for copy, out, at in zip(copies, back, parts):
         copy.wait()
         scale = held[F : F + 16, at].astype(jnp.float32)[0:1, :] * (1.0 / TOP)
         for row in range(0, F, 16):
             total[row : row + 16, at] = decode(held[row : row + 16, at], scale)
         out.start()
-        if at is parts[0]:
-            for arrive, leave in zip(ins, outs):
-                arrive.wait()
-                leave.start()
     for copy in outs + back:
         copy.wait()
 

time: 96.8 us -> 96.9 us (level)
  no operation moved by 1% of the time
where the time goes in v6:
time: 96.9 us; the launch traced here: 96.3 us
  Pallas kernels  95.7 us (99%)
    pallas_call x1, Pallas kernels, shards(): pl.pallas_call(kernel, out_shape=(jax.ShapeDtypeStruct(hidden.shape, jnp....  92.9 us
    pallas_call x1, Pallas kernels, shards(): pl.pallas_call(finish, out_shape=(jax.ShapeDtypeStruct(hidden.shape, jnp....  2.81 us

profile of v6, /device:TPU:1, one launch (start us, length us, event | category | flops | bytes accessed | tf_op | source)
XLA Modules:
  0.0 96.3 jit_solution(2321690124068564322)
XLA Ops:
  0.6 92.9 %shard_map.50 = (bf16[160,3584]{1,0:T(8,128)(2,1)}, bf16[80,3584]{1,0:T(8,128)(2,1)}) custom-call(bf16[160,3584]{1,0:T(8,128)(2,1)} %hidden.1, bf16[160,1024]{1,0:T(8,128)(2,1)} %grad.1, bf16[64,3584]{1,0:T(8,128)(2,1)} %weight.1), custom_call_target="tpu_custom_call" | custom-call | tf_op jit(solution)/shard_map/pallas_call | solution.py:511
  93.5 2.8 %shard_map.51 = (bf16[160,3584]{1,0:T(8,128)(2,1)}, f32[64,3584]{1,0:T(8,128)}) custom-call(bf16[160,3584]{1,0:T(8,128)(2,1)} %get-tuple-element.4.hg, bf16[80,3584]{1,0:T(8,128)(2,1)} %get-tuple-element.5.code), custom_call_target="tpu_custom_call" | custom-call | tf_op jit(solution)/shard_map/pallas_call | solution.py:544
